TPU v7x, 512 devices: a whole 4x8x8 slice. The times are simulated.
512 devices in a mesh: row: 32 (over x, y), col: 16 (over z, core).
Axes of the slice: x: 4, y: 8, z: 8, core: 2. Of those that a mesh axis runs over, the one named last changes fastest.
Arguments:
- right_side: bfloat16 [5, 8, 512, 2048], P(None, None, 'row', 'col'), as said below
- near_bands: bfloat16 [3, 2, 8, 512, 2048], P(None, None, None, 'row', 'col'), as said below
- margins: bfloat16 [3, 8, 512, 2048], P(None, None, 'row', 'col'), as said below
Outputs:
- update: float32 [5, 8, 512, 2048], P(None, None, 'row', 'col')
Inputs may be any that keep to these rules, and one draw needn't show every extreme that they name: `right_side`: every entry has magnitude at most 2 (2048)^(-3/2). `near_bands`: every entry lies between -0.9 and -0.2. `margins`: every entry is positive and at most 2.
All inputs are finite; a program needn't handle non-finite values.
Results may differ from a plain program's by a relative error of at most 0.005.
Values sent between devices are 32-bit elements; how exact they have to be, the bound alone decides.
No kernel may reach another device: no remote copies, remote signals or barrier semaphores. Data moves between devices by JAX's collectives and lax.ppermute only.
A program may use at most 192 MiB of HBM per device.

v0:
```python
import jax
import jax.numpy as jnp
from jax import lax
from jax.experimental import pallas as pl
from jax.experimental.pallas import tpu as pltpu
from jax.sharding import PartitionSpec as P

VARS = 5
OUTER = 0.05
F32 = jnp.float32
PARAMS = pltpu.CompilerParams(vmem_limit_bytes=48 * 1024 * 1024)

HEAD, TAIL, HEAD_IN, TAIL_IN, HEAD_OUT, TAIL_OUT = 0, 10, 20, 24, 28, 32


def solve_block(below, middle, above, sources, cells):
    count = len(sources[0])
    ratio_one, ratio_two, reduced = [], [], []
    for i in range(cells):
        sub, mid, sup = below(i), middle(i), above(i)
        zero = jnp.zeros_like(mid)
        lower = sub + OUTER * ratio_one[i - 2] if i >= 2 else sub
        centre = mid + OUTER * ratio_two[i - 2] if i >= 2 else mid
        upper = sup
        if i >= 1:
            centre = centre - lower * ratio_one[i - 1]
            upper = sup - lower * ratio_two[i - 1]
        inverse = 1.0 / centre
        row = list(sources[i])
        row.append(zero - OUTER if i == 0 else zero)
        row.append(sub if i == 0 else zero - OUTER if i == 1 else zero)
        new = []
        for c in range(count + 2):
            value = row[c]
            if i >= 2:
                value = value + OUTER * reduced[i - 2][c]
            if i >= 1:
                value = value - lower * reduced[i - 1][c]
            new.append(value * inverse)
        if i == cells - 2:
            new += [-OUTER * inverse, zero]
        elif i == cells - 1:
            new += [(sup - lower * reduced[i - 1][count + 2]) * inverse, -OUTER * inverse]
        reduced.append(new)
        ratio_one.append(upper * inverse)
        ratio_two.append(-OUTER * inverse)
    solved = [None] * cells
    solved[cells - 1] = reduced[cells - 1]
    for i in range(cells - 2, -1, -1):
        out = []
        for c in range(count + 4):
            value = reduced[i][c] if c < len(reduced[i]) else None
            term = ratio_one[i] * solved[i + 1][c]
            value = -term if value is None else value - term
            if i + 2 < cells:
                value = value - ratio_two[i] * solved[i + 2][c]
            out.append(value)
        solved[i] = out
    return solved


def relation_of(solved):
    first, second, before, last = solved[0], solved[1], solved[-2], solved[-1]
    relation = []
    for pair in ((first, second), (before, last)):
        for cell in pair:
            relation += cell[:VARS]
    for lo in (VARS, VARS + 2):
        for pair in ((first, second), (before, last)):
            for cell in pair:
                relation += cell[lo : lo + 2]
    return relation


def product(left, right):
    wide = len(right) // 2
    return [
        left[2 * r] * right[c] + left[2 * r + 1] * right[wide + c] for r in range(2) for c in range(wide)
    ]


def plus(a, b):
    return [x + y for x, y in zip(a, b)]


def minus(a, b):
    return [x - y for x, y in zip(a, b)]


def parts(relation):
    return (
        relation[HEAD:TAIL],
        relation[TAIL:HEAD_IN],
        relation[HEAD_IN:TAIL_IN],
        relation[TAIL_IN:HEAD_OUT],
        relation[HEAD_OUT:TAIL_OUT],
        relation[TAIL_OUT:],
    )


def merge(left, right):
    hv_a, tv_a, hin_a, tin_a, hout_a, tout_a = parts(left)
    hv_b, tv_b, hin_b, tin_b, hout_b, tout_b = parts(right)
    loop = product(tout_a, hin_b)
    a, b, c, d = 1.0 - loop[0], -loop[1], -loop[2], 1.0 - loop[3]
    inverse = 1.0 / (a * d - b * c)
    shift = [d * inverse, -b * inverse, -c * inverse, a * inverse]
    jv = product(shift, minus(tv_a, product(tout_a, hv_b)))
    jp = product(shift, tin_a)
    jf = product(shift, product(tout_a, hout_b))
    kv = minus(hv_b, product(hin_b, jv))
    kp = product(hin_b, jp)
    kf = plus(product(hin_b, jf), hout_b)
    merged = (
        minus(hv_a, product(hout_a, kv))
        + minus(tv_b, product(tin_b, jv))
        + plus(hin_a, product(hout_a, kp))
        + [-x for x in product(tin_b, jp)]
        + [-x for x in product(hout_a, kf)]
        + plus(product(tin_b, jf), tout_b)
    )
    return merged, jv + kv + jp + jf + kp + kf


def joint(saved, prev, following):
    jv, kv, jp, jf, kp, kf = saved[:10], saved[10:20], saved[20:24], saved[24:28], saved[28:32], saved[32:]
    tail = plus(minus(jv, product(jp, prev)), product(jf, following))
    head = minus(plus(kv, product(kp, prev)), product(kf, following))
    return tail, head


def rolled(values, shift, axis):
    return [pltpu.roll(v, shift, axis) for v in values]


def climb(relation, levels):
    kept = []
    for axis, distance, size in levels:
        relation, saved = merge(relation, rolled(relation, size - distance, axis))
        kept.append(saved)
    return relation, kept


def descend(kept, levels, prev, following):
    for saved, (axis, distance, size) in zip(reversed(kept), reversed(levels)):
        tail, head = joint(saved, prev, following)
        place = lax.broadcasted_iota(jnp.int32, (8, 128), axis)
        is_right = (place & distance) != 0
        prev = [jnp.where(is_right, pltpu.roll(t, distance, axis), p) for t, p in zip(tail, prev)]
        following = [jnp.where(is_right, pltpu.roll(f, distance, axis), h) for f, h in zip(following, head)]
    return prev, following


def swap_quarters(four):
    lane = lax.broadcasted_iota(jnp.int32, (8, 128), 1)
    low_two, low_one = (lane & 64) == 0, (lane & 32) == 0
    half = [None] * 4
    for j in (0, 1):
        a, b = four[j], four[j + 2]
        half[j] = jnp.where(low_two, a, pltpu.roll(b, 64, 1))
        half[j + 2] = jnp.where(low_two, pltpu.roll(a, 64, 1), b)
    out = [None] * 4
    for j in (0, 2):
        a, b = half[j], half[j + 1]
        out[j] = jnp.where(low_one, a, pltpu.roll(b, 32, 1))
        out[j + 1] = jnp.where(low_one, pltpu.roll(a, 96, 1), b)
    return out


ROW_LEVELS = ((1, 32, 128), (1, 64, 128), (0, 1, 8), (0, 2, 8), (0, 4, 8))
SUB_LEVELS = ((0, 1, 8), (0, 2, 8), (0, 4, 8))


def bands_of(bands_ref, margins_ref, direction):
    below = bands_ref[direction, 0].astype(F32)
    above = bands_ref[direction, 1].astype(F32)
    middle = jnp.abs(below) + jnp.abs(above) + 0.1 + margins_ref[direction].astype(F32)
    return below, middle, above


def x_local(right_ref, bands_ref, margins_ref, solved_ref, sent_ref, lines):
    below, middle, above = bands_of(bands_ref, margins_ref, 0)
    for slot, array in enumerate((below, middle, above)):
        lines[slot] = array.reshape(128, 128)
    for v in range(VARS):
        lines[3 + v] = right_ref[v].astype(F32).reshape(128, 128)

    def cell(slot):
        return lambda i: lines[slot, pl.ds(i, 8, stride=16), :]

    sources = [[cell(3 + v)(i) for v in range(VARS)] for i in range(16)]
    solved = solve_block(cell(0), cell(1), cell(2), sources, 16)
    for i in range(16):
        for c in range(VARS + 4):
            solved_ref[i, c] = solved[i][c]
    relation = relation_of(solved)
    for g in range(9):
        out = swap_quarters(relation[4 * g : 4 * g + 4])
        for quarter in range(4):
            sent_ref[pl.ds(quarter * 16 + g, 8, stride=64), :] = out[quarter]


def x_join(got_ref, sent_ref):
    relation = []
    for g in range(9):
        relation += swap_quarters([got_ref[pl.ds(quarter * 16 + g, 8, stride=64), :] for quarter in range(4)])
    _, kept = climb(relation, ROW_LEVELS)
    zero = [jnp.zeros((8, 128), F32)] * 10
    prev, following = descend(kept, ROW_LEVELS, zero, zero)
    answer = prev + following
    for g in range(5):
        out = swap_quarters(answer[4 * g : 4 * g + 4])
        for quarter in range(4):
            sent_ref[pl.ds(quarter * 8 + g, 8, stride=32), :] = out[quarter]


def with_neighbours(cell, prev, following):
    before_one, before_two, after_one, after_two = cell[VARS:]
    return [
        cell[v]
        - before_one * prev[v]
        - before_two * prev[VARS + v]
        - after_one * following[v]
        - after_two * following[VARS + v]
        for v in range(VARS)
    ]


def y_local(x_solved_ref, got_ref, bands_ref, margins_ref, solved_ref, kept_ref, sent_ref, lines, row):
    answer = []
    for g in range(5):
        answer += swap_quarters([got_ref[pl.ds(quarter * 8 + g, 8, stride=32), :] for quarter in range(4)])
    prev, following = answer[:10], answer[10:]
    for i in range(16):
        cell = [x_solved_ref[i, c] for c in range(VARS + 4)]
        for v, value in enumerate(with_neighbours(cell, prev, following)):
            lines[3 + v, pl.ds(i, 8, stride=16), :] = value
    for slot, array in enumerate(bands_of(bands_ref, margins_ref, 1)):
        lines[slot] = array.reshape(128, 128).T
    for v in range(VARS):
        lines[3 + v] = lines[3 + v].T

    def cell_of(slot):
        return lambda i: lines[slot, pl.ds(i, 8, stride=16), :]

    sources = [[cell_of(3 + v)(i) for v in range(VARS)] for i in range(16)]
    solved = solve_block(cell_of(0), cell_of(1), cell_of(2), sources, 16)
    for i in range(16):
        for c in range(VARS + 4):
            solved_ref[i, c] = solved[i][c]
    relation, kept = climb(relation_of(solved), SUB_LEVELS)
    for level in range(3):
        for c in range(36):
            kept_ref[level, c] = kept[level][c]
    for c in range(36):
        row[c : c + 1, :] = relation[c][0:1, :]
    whole = row[...]
    for j in range(16):
        sent_ref[pl.ds(j * 40, 40), :] = whole


def y_join(got_ref, y_solved_ref, kept_ref, bands_ref, margins_ref, out_ref, lines, row):
    mine = lax.axis_index("col")
    even = [got_ref[pl.ds(c, 8, stride=80), :] for c in range(36)]
    odd = [got_ref[pl.ds(40 + c, 8, stride=80), :] for c in range(36)]
    relation, pair = merge(even, odd)
    _, kept = climb(relation, SUB_LEVELS)
    zero = [jnp.zeros((8, 128), F32)] * 10
    prev, following = descend(kept, SUB_LEVELS, zero, zero)
    tail, head = joint(pair, prev, following)
    is_odd = jnp.full((8, 128), mine % 2, jnp.int32) != 0
    prev = [jnp.where(is_odd, t, p) for t, p in zip(tail, prev)]
    following = [jnp.where(is_odd, f, h) for f, h in zip(following, head)]
    for c, value in enumerate(prev + following):
        row[c] = value
    place = mine // 2
    own = [jnp.broadcast_to(row[c, pl.ds(place, 1), :], (8, 128)) for c in range(20)]
    kept = [[kept_ref[level, c] for c in range(36)] for level in range(3)]
    prev, following = descend(kept, SUB_LEVELS, own[:10], own[10:])
    for i in range(16):
        cell = [y_solved_ref[i, c] for c in range(VARS + 4)]
        for v, value in enumerate(with_neighbours(cell, prev, following)):
            lines[v, pl.ds(i, 8, stride=16), :] = value
    below, middle, above = bands_of(bands_ref, margins_ref, 2)
    ratio_one, ratio_two, reduced = [], [], []
    fields = [lines[v].T.reshape(8, 16, 128) for v in range(VARS)]
    for i in range(8):
        lower = below[i] + OUTER * ratio_one[i - 2] if i >= 2 else below[i]
        centre = middle[i] + OUTER * ratio_two[i - 2] if i >= 2 else middle[i]
        upper = above[i]
        if i >= 1:
            centre = centre - lower * ratio_one[i - 1]
            upper = upper - lower * ratio_two[i - 1]
        inverse = 1.0 / centre
        new = []
        for v in range(VARS):
            value = fields[v][i]
            if i >= 2:
                value = value + OUTER * reduced[i - 2][v]
            if i >= 1:
                value = value - lower * reduced[i - 1][v]
            new.append(value * inverse)
        reduced.append(new)
        ratio_one.append(upper * inverse)
        ratio_two.append(-OUTER * inverse)
    later = [None, None]
    for i in range(7, -1, -1):
        now = []
        for v in range(VARS):
            value = reduced[i][v]
            if later[0] is not None:
                value = value - ratio_one[i] * later[0][v]
            if later[1] is not None:
                value = value - ratio_two[i] * later[1][v]
            now.append(value)
            out_ref[v, i] = value
        later = [now, later[0]]


def call(kernel, outs, scratch):
    return pl.pallas_call(
        kernel,
        out_shape=[jax.ShapeDtypeStruct(shape, F32) for shape in outs],
        scratch_shapes=[pltpu.VMEM(shape, F32) for shape in scratch],
        compiler_params=PARAMS,
    )


def exchange(array, axis, count):
    array = array.reshape(count, -1, 128)
    return lax.all_to_all(array, axis, 0, 0, tiled=True).reshape(-1, 128)


def body(right_side, near_bands, margins):
    x_solved, sent = call(x_local, [(16, 9, 8, 128), (512, 128)], [(8, 128, 128)])(
        right_side, near_bands, margins
    )
    (answer,) = call(x_join, [(256, 128)], [])(exchange(sent, "row", 32))
    y_solved, kept, sent = call(
        y_local, [(16, 9, 8, 128), (3, 36, 8, 128), (640, 128)], [(8, 128, 128), (40, 128)]
    )(x_solved, exchange(answer, "row", 32), near_bands, margins)
    (update,) = call(y_join, [(VARS, 8, 16, 128)], [(VARS, 128, 128), (20, 8, 128)])(
        exchange(sent, "col", 16), y_solved, kept, near_bands, margins
    )
    return update


def solution(mesh):
    placed = (
        P(None, None, "row", "col"),
        P(None, None, None, "row", "col"),
        P(None, None, "row", "col"),
    )
    return jax.shard_map(
        body, mesh=mesh, in_specs=placed, out_specs=P(None, None, "row", "col"), check_vma=False
    )
```

profile of v0, /device:TPU:1, one launch (start us, length us, event | category | flops | bytes accessed | tf_op | source)
XLA Modules:
  0.0 68.0 jit_solution(10419422154444983597)
XLA Ops:
  0.0 0.0 copy-start
  0.0 0.9 %copy-done = bf16[3,2,8,16,128]{4,3,2,1,0:T(8,128)(2,1)S(1)} copy-done((bf16[3,2,8,16,128]{4,3,2,1,0:T(8,128)(2,1)S(1)}, bf16[3,2,8,16,128]{4,3,2,1,0:T(8,128)(2,1)}, u32[]{:S(2)}) %copy-start) | copy-done | bytes 196632
  0.9 0.0 copy-start.2
  0.9 0.9 %copy-done.2 = bf16[3,8,16,128]{3,2,1,0:T(8,128)(2,1)S(1)} copy-done((bf16[3,8,16,128]{3,2,1,0:T(8,128)(2,1)S(1)}, bf16[3,8,16,128]{3,2,1,0:T(8,128)(2,1)}, u32[]{:S(2)}) %copy-start.2) | copy-done | bytes 98328
  1.8 0.0 copy-start.4
  1.8 0.9 %copy-done.4 = bf16[5,8,16,128]{3,2,1,0:T(8,128)(2,1)S(1)} copy-done((bf16[5,8,16,128]{3,2,1,0:T(8,128)(2,1)S(1)}, bf16[5,8,16,128]{3,2,1,0:T(8,128)(2,1)}, u32[]{:S(2)}) %copy-start.4) | copy-done | bytes 163864
  2.7 0.5 shard_map.37
  3.2 20.0 %all_to_all.15 = f32[32,16,128]{2,1,0:T(8,128)S(1)} all-to-all(f32[32,16,128]{2,1,0:T(8,128)S(1)} %bitcast.11), channel_id=1, replica_groups=mesh['row'=32,'col'=16] {'row'}, dimensions={0} | all-to-all | bytes 524288 | tf_op jit(solution)/shard_map/all_to_all | solution.py:331
  23.2 0.0 copy-start.3
  23.2 0.9 %shard_map.38 = f32[256,128]{1,0:T(8,128)S(1)} custom-call(f32[512,128]{1,0:T(8,128)S(1)} %bitcast.7), custom_call_target="tpu_custom_call" | custom-call | tf_op jit(solution)/shard_map/pallas_call | solution.py:338
  24.1 0.0 copy-start.1
  24.2 15.4 %all_to_all.16 = f32[32,8,128]{2,1,0:T(8,128)S(1)} all-to-all(f32[32,8,128]{2,1,0:T(8,128)S(1)} %bitcast.8), channel_id=1, replica_groups=mesh['row'=32,'col'=16] {'row'}, dimensions={0} | all-to-all | bytes 262144 | tf_op jit(solution)/shard_map/all_to_all | solution.py:331
  39.5 0.0 copy-done.3
  39.5 0.0 copy-done.1
  39.5 0.8 %shard_map.39 = (f32[16,9,8,128]{3,2,1,0:T(8,128)S(1)}, f32[3,36,8,128]{3,2,1,0:T(8,128)S(1)}, f32[640,128]{1,0:T(8,128)S(1)}) custom-call(f32[16,9,8,128]{3,2,1,0:T(8,128)S(1)} %get-tuple-element.10.x_solved_ref, f32[256,128]{1,0:T(8,128)S(1)} %bitcast.9, bf16[3,2,8,16,128]{4,3,2,1,0:T(8,128)(2,1)S(1)} %copy-done.1, bf16[3,8,16,128]{3,2,1,0:T(8,128)(2,1)S(1)} %copy-done.3), custom_call_target="tpu_custom_call" | custom-call | tf_op jit(solution)/shard_map/pallas_call | solution.py:339
  40.3 26.3 %all_to_all.17 = f32[16,40,128]{2,1,0:T(8,128)S(1)} all-to-all(f32[16,40,128]{2,1,0:T(8,128)S(1)} %bitcast.10), channel_id=1, replica_groups=mesh['row'=32,'col'=16] {'col'}, dimensions={0} | all-to-all | bytes 655360 | tf_op jit(solution)/shard_map/all_to_all | solution.py:331
  66.6 1.4 %shard_map.40 = f32[5,8,16,128]{3,2,1,0:T(8,128)} custom-call(f32[640,128]{1,0:T(8,128)S(1)} %bitcast.6, f32[16,9,8,128]{3,2,1,0:T(8,128)S(1)} %get-tuple-element.13.y_solved_ref, f32[3,36,8,128]{3,2,1,0:T(8,128)S(1)} %get-tuple-element.14.kept_ref, bf16[3,2,8,16,128]{4,3,2,1,0:T(8,128)(2,1)S(1)} %copy-done.1, bf16[3,8,16,128]{3,2,1,0:T(8,128)(2,1)S(1)} %copy-done.3), custom_call_target="tpu_custom_call" | custom-call | tf_op jit(solution)/shard_map/pallas_call | solution.py:342
Async XLA Ops:
  0.0 0.9 %copy-start = (bf16[3,2,8,16,128]{4,3,2,1,0:T(8,128)(2,1)S(1)}, bf16[3,2,8,16,128]{4,3,2,1,0:T(8,128)(2,1)}, u32[]{:S(2)}) copy-start(bf16[3,2,8,16,128]{4,3,2,1,0:T(8,128)(2,1)} %bands_ref.5) | copy-start | bytes 589828
  0.9 0.9 %copy-start.2 = (bf16[3,8,16,128]{3,2,1,0:T(8,128)(2,1)S(1)}, bf16[3,8,16,128]{3,2,1,0:T(8,128)(2,1)}, u32[]{:S(2)}) copy-start(bf16[3,8,16,128]{3,2,1,0:T(8,128)(2,1)} %margins_ref.5) | copy-start | bytes 294916
  1.8 0.9 %copy-start.4 = (bf16[5,8,16,128]{3,2,1,0:T(8,128)(2,1)S(1)}, bf16[5,8,16,128]{3,2,1,0:T(8,128)(2,1)}, u32[]{:S(2)}) copy-start(bf16[5,8,16,128]{3,2,1,0:T(8,128)(2,1)} %right_ref.1) | copy-start | bytes 491524
  23.2 16.3 %copy-start.3 = (bf16[3,8,16,128]{3,2,1,0:T(8,128)(2,1)S(1)}, bf16[3,8,16,128]{3,2,1,0:T(8,128)(2,1)}, u32[]{:S(2)}) copy-start(bf16[3,8,16,128]{3,2,1,0:T(8,128)(2,1)} %margins_ref.5) | copy-start | bytes 294916
  24.1 15.4 %copy-start.1 = (bf16[3,2,8,16,128]{4,3,2,1,0:T(8,128)(2,1)S(1)}, bf16[3,2,8,16,128]{4,3,2,1,0:T(8,128)(2,1)}, u32[]{:S(2)}) copy-start(bf16[3,2,8,16,128]{4,3,2,1,0:T(8,128)(2,1)} %bands_ref.5) | copy-start | bytes 589828
where the time goes:
time: 68.3 us; the launch traced here: 68 us
  blocking collectives  61.6 us (90%)
  Pallas kernels  3.63 us (5%)
  local copies, waits for them, and re-layouts  2.74 us (4%)
    all_to_all x3, blocking collectives, exchange(): return lax.all_to_all(array, axis, 0, 0, tiled=True).reshape(-1, 128)  61.6 us
    unnamed x10, local copies, waits for them, and re-layouts  2.74 us
    pallas_call x1, Pallas kernels, body(): call(y_join, [(VARS, 8, 16, 128)], [(VARS, 128, 128), (20, 8, 128)])  1.45 us

commit v1 on v0

--- a/solution.py
+++ b/solution.py
@@ -151,23 +151,13 @@
     return prev, following
 
 
-def swap_quarters(four):
-    lane = lax.broadcasted_iota(jnp.int32, (8, 128), 1)
-    low_two, low_one = (lane & 64) == 0, (lane & 32) == 0
-    half = [None] * 4
-    for j in (0, 1):
-        a, b = four[j], four[j + 2]
-        half[j] = jnp.where(low_two, a, pltpu.roll(b, 64, 1))
-        half[j + 2] = jnp.where(low_two, pltpu.roll(a, 64, 1), b)
-    out = [None] * 4
-    for j in (0, 2):
-        a, b = half[j], half[j + 1]
-        out[j] = jnp.where(low_one, a, pltpu.roll(b, 32, 1))
-        out[j + 1] = jnp.where(low_one, pltpu.roll(a, 96, 1), b)
-    return out
-
-
-ROW_LEVELS = ((1, 32, 128), (1, 64, 128), (0, 1, 8), (0, 2, 8), (0, 4, 8))
+RING_ORDER, ACROSS_ORDER, DEEP_ORDER = (4, 3, 5, 2, 6, 1, 7, 0), (2, 1, 3, 0), (6, 7, 5, 4, 3, 2, 1, 0)
+RING = [[8 * x + y for y in RING_ORDER] for x in range(4)]
+ACROSS = [[8 * x + y for x in ACROSS_ORDER] for y in range(8)]
+DEEP = [[2 * z + core for z in DEEP_ORDER] for core in range(2)]
+CORES = [[2 * z, 2 * z + 1] for z in range(8)]
+
+FOUR_LEVELS = ((0, 1, 8), (0, 2, 8))
 SUB_LEVELS = ((0, 1, 8), (0, 2, 8), (0, 4, 8))
 
 
@@ -178,12 +168,23 @@
     return below, middle, above
 
 
-def x_local(right_ref, bands_ref, margins_ref, solved_ref, sent_ref, lines):
-    below, middle, above = bands_of(bands_ref, margins_ref, 0)
+def x_local(right_hbm, bands_hbm, margins_hbm, solved_ref, sent_ref, lines, right, bands, margins, arrived):
+    copies = [
+        pltpu.make_async_copy(bands_hbm.at[0], bands, arrived.at[0]),
+        pltpu.make_async_copy(margins_hbm.at[0], margins, arrived.at[1]),
+        pltpu.make_async_copy(right_hbm, right, arrived.at[2]),
+    ]
+    for copy in copies:
+        copy.start()
+    copies[0].wait()
+    copies[1].wait()
+    below, above = bands[0].astype(F32), bands[1].astype(F32)
+    middle = jnp.abs(below) + jnp.abs(above) + 0.1 + margins[...].astype(F32)
     for slot, array in enumerate((below, middle, above)):
         lines[slot] = array.reshape(128, 128)
+    copies[2].wait()
     for v in range(VARS):
-        lines[3 + v] = right_ref[v].astype(F32).reshape(128, 128)
+        lines[3 + v] = right[v].astype(F32).reshape(128, 128)
 
     def cell(slot):
         return lambda i: lines[slot, pl.ds(i, 8, stride=16), :]
@@ -194,24 +195,54 @@
         for c in range(VARS + 4):
             solved_ref[i, c] = solved[i][c]
     relation = relation_of(solved)
-    for g in range(9):
-        out = swap_quarters(relation[4 * g : 4 * g + 4])
-        for quarter in range(4):
-            sent_ref[pl.ds(quarter * 16 + g, 8, stride=64), :] = out[quarter]
-
-
-def x_join(got_ref, sent_ref):
-    relation = []
-    for g in range(9):
-        relation += swap_quarters([got_ref[pl.ds(quarter * 16 + g, 8, stride=64), :] for quarter in range(4)])
-    _, kept = climb(relation, ROW_LEVELS)
+    for c in range(36):
+        sent_ref[pl.ds(c, 8, stride=40), :] = relation[c]
+
+
+def send_to_all(relation, sent_ref, row, count):
+    row[...] = jnp.zeros_like(row)
+    for c in range(36):
+        row[c : c + 1, :] = relation[c][0:1, :]
+    whole = row[...]
+    for j in range(count):
+        sent_ref[pl.ds(j * 40, 40), :] = whole
+
+
+def own_part(values, place, row):
+    for c, value in enumerate(values):
+        row[c] = value
+    return [jnp.broadcast_to(row[c, pl.ds(place, 1), :], (8, 128)) for c in range(len(values))]
+
+
+def in_order(got_ref, ordered, order):
+    for position, member in enumerate(order):
+        ordered[member * 40 : member * 40 + 40, :] = got_ref[position * 40 : position * 40 + 40, :]
+    return [ordered[pl.ds(c, 8, stride=40), :] for c in range(36)]
+
+
+def x_ring(got_ref, kept_ref, sent_ref, row, ordered):
+    relation, kept = climb(in_order(got_ref, ordered, RING_ORDER), SUB_LEVELS)
+    for level in range(3):
+        for c in range(36):
+            kept_ref[level, c] = kept[level][c]
+    send_to_all(relation, sent_ref, row, 4)
+
+
+def x_join(got_ref, kept_ref, sent_ref, twice, row, ordered):
+    for half in range(2):
+        for position, member in enumerate(ACROSS_ORDER):
+            start = half * 160 + member * 40
+            twice[start : start + 40, :] = got_ref[position * 40 : position * 40 + 40, :]
+    _, kept = climb([twice[pl.ds(c, 8, stride=40), :] for c in range(36)], FOUR_LEVELS)
     zero = [jnp.zeros((8, 128), F32)] * 10
-    prev, following = descend(kept, ROW_LEVELS, zero, zero)
-    answer = prev + following
-    for g in range(5):
-        out = swap_quarters(answer[4 * g : 4 * g + 4])
-        for quarter in range(4):
-            sent_ref[pl.ds(quarter * 8 + g, 8, stride=32), :] = out[quarter]
+    prev, following = descend(kept, FOUR_LEVELS, zero, zero)
+    own = own_part(prev + following, lax.axis_index("row") // 8, row)
+    kept = [[kept_ref[level, c] for c in range(36)] for level in range(3)]
+    prev, following = descend(kept, SUB_LEVELS, own[:10], own[10:])
+    for c, value in enumerate(prev + following):
+        ordered[pl.ds(c, 8, stride=24), :] = value
+    for position, member in enumerate(RING_ORDER):
+        sent_ref[position * 24 : position * 24 + 24, :] = ordered[member * 24 : member * 24 + 24, :]
 
 
 def with_neighbours(cell, prev, following):
@@ -227,9 +258,7 @@
 
 
 def y_local(x_solved_ref, got_ref, bands_ref, margins_ref, solved_ref, kept_ref, sent_ref, lines, row):
-    answer = []
-    for g in range(5):
-        answer += swap_quarters([got_ref[pl.ds(quarter * 8 + g, 8, stride=32), :] for quarter in range(4)])
+    answer = [got_ref[pl.ds(c, 8, stride=24), :] for c in range(20)]
     prev, following = answer[:10], answer[10:]
     for i in range(16):
         cell = [x_solved_ref[i, c] for c in range(VARS + 4)]
@@ -252,29 +281,28 @@
     for level in range(3):
         for c in range(36):
             kept_ref[level, c] = kept[level][c]
+    send_to_all(relation, sent_ref, row, 1)
+
+
+def y_pair(got_ref, pair_ref, sent_ref, row):
+    left, right = ([got_ref[40 * s + c : 40 * s + c + 1, :] for c in range(36)] for s in range(2))
+    relation, pair = merge(left, right)
     for c in range(36):
-        row[c : c + 1, :] = relation[c][0:1, :]
-    whole = row[...]
-    for j in range(16):
-        sent_ref[pl.ds(j * 40, 40), :] = whole
-
-
-def y_join(got_ref, y_solved_ref, kept_ref, bands_ref, margins_ref, out_ref, lines, row):
+        pair_ref[c : c + 1, :] = pair[c]
+    send_to_all(relation, sent_ref, row, 8)
+
+
+def y_join(got_ref, pair_ref, y_solved_ref, kept_ref, bands_ref, margins_ref, out_ref, lines, row, ordered):
     mine = lax.axis_index("col")
-    even = [got_ref[pl.ds(c, 8, stride=80), :] for c in range(36)]
-    odd = [got_ref[pl.ds(40 + c, 8, stride=80), :] for c in range(36)]
-    relation, pair = merge(even, odd)
-    _, kept = climb(relation, SUB_LEVELS)
+    _, kept = climb(in_order(got_ref, ordered, DEEP_ORDER), SUB_LEVELS)
     zero = [jnp.zeros((8, 128), F32)] * 10
     prev, following = descend(kept, SUB_LEVELS, zero, zero)
-    tail, head = joint(pair, prev, following)
-    is_odd = jnp.full((8, 128), mine % 2, jnp.int32) != 0
-    prev = [jnp.where(is_odd, t, p) for t, p in zip(tail, prev)]
-    following = [jnp.where(is_odd, f, h) for f, h in zip(following, head)]
-    for c, value in enumerate(prev + following):
-        row[c] = value
-    place = mine // 2
-    own = [jnp.broadcast_to(row[c, pl.ds(place, 1), :], (8, 128)) for c in range(20)]
+    own = own_part(prev + following, mine // 2, row)
+    prev, following = own[:10], own[10:]
+    tail, head = joint([pair_ref[c : c + 1, :] for c in range(36)], prev, following)
+    is_right = jnp.full((8, 128), mine % 2, jnp.int32) != 0
+    own = [jnp.where(is_right, t, p) for t, p in zip(tail, prev)]
+    own += [jnp.where(is_right, f, h) for f, h in zip(following, head)]
     kept = [[kept_ref[level, c] for c in range(36)] for level in range(3)]
     prev, following = descend(kept, SUB_LEVELS, own[:10], own[10:])
     for i in range(16):
@@ -326,21 +354,34 @@
     )
 
 
-def exchange(array, axis, count):
+def exchange(array, axis, count, members=None):
     array = array.reshape(count, -1, 128)
-    return lax.all_to_all(array, axis, 0, 0, tiled=True).reshape(-1, 128)
+    return lax.all_to_all(array, axis, 0, 0, tiled=True, axis_index_groups=members).reshape(-1, 128)
 
 
 def body(right_side, near_bands, margins):
-    x_solved, sent = call(x_local, [(16, 9, 8, 128), (512, 128)], [(8, 128, 128)])(
-        right_side, near_bands, margins
-    )
-    (answer,) = call(x_join, [(256, 128)], [])(exchange(sent, "row", 32))
+    x_solved, sent = pl.pallas_call(
+        x_local,
+        in_specs=[pl.BlockSpec(memory_space=pltpu.HBM)] * 3,
+        out_shape=[jax.ShapeDtypeStruct((16, 9, 8, 128), F32), jax.ShapeDtypeStruct((320, 128), F32)],
+        scratch_shapes=[
+            pltpu.VMEM((8, 128, 128), F32),
+            pltpu.VMEM((VARS, 8, 16, 128), jnp.bfloat16),
+            pltpu.VMEM((2, 8, 16, 128), jnp.bfloat16),
+            pltpu.VMEM((8, 16, 128), jnp.bfloat16),
+            pltpu.SemaphoreType.DMA((3,)),
+        ],
+        compiler_params=PARAMS,
+    )(*[pltpu.with_memory_space_constraint(a, pltpu.HBM) for a in (right_side, near_bands, margins)])
+    kept, sent = call(x_ring, [(3, 36, 8, 128), (160, 128)], [(40, 128), (320, 128)])(exchange(sent, "row", 8, RING))
+    (answer,) = call(x_join, [(192, 128)], [(320, 128), (20, 8, 128), (192, 128)])(exchange(sent, "row", 4, ACROSS), kept)
     y_solved, kept, sent = call(
-        y_local, [(16, 9, 8, 128), (3, 36, 8, 128), (640, 128)], [(8, 128, 128), (40, 128)]
-    )(x_solved, exchange(answer, "row", 32), near_bands, margins)
-    (update,) = call(y_join, [(VARS, 8, 16, 128)], [(VARS, 128, 128), (20, 8, 128)])(
-        exchange(sent, "col", 16), y_solved, kept, near_bands, margins
+        y_local, [(16, 9, 8, 128), (3, 36, 8, 128), (40, 128)], [(8, 128, 128), (40, 128)]
+    )(x_solved, exchange(answer, "row", 8, RING), near_bands, margins)
+    both = lax.all_gather(sent, "col", axis_index_groups=CORES, tiled=True)
+    pair, sent = call(y_pair, [(36, 128), (320, 128)], [(40, 128)])(both)
+    (update,) = call(y_join, [(VARS, 8, 16, 128)], [(VARS, 128, 128), (20, 8, 128), (320, 128)])(
+        exchange(sent, "col", 8, DEEP), pair, y_solved, kept, near_bands, margins
     )
     return update
 

time: 68.3 us -> 54.8 us (0.80)
  blocking collectives: 61.6 us -> 50.1 us
  local copies, waits for them, and re-layouts: 2.74 us -> 0.01 us
    all_to_all x3 -> x4, blocking collectives: 61.6 us -> 41.6 us  [exchange(): lax.all_to_all(array, axis, 0, 0, tiled=True, axis_index_groups=members)]
    all_gather x0 -> x1, blocking collectives: none -> 8.5 us  [body(): both = lax.all_gather(sent, 'col', axis_index_groups=CORES, tiled=True)]
    unnamed x10 -> x4, local copies, waits for them, and re-layouts: 2.74 us -> 0.01 us
    pallas_call x4 -> x6, Pallas kernels: 3.63 us -> 3.91 us  [the longest x1 1.36 us: body(): call(y_join, [(VARS, 8, 16, 128)], [(VARS, 128, 128), (20, 8, 128), (320,...]
where the time goes in v1:
time: 54.8 us; the launch traced here: 54 us
  blocking collectives  50.1 us (91%)
  Pallas kernels  3.91 us (7%)
    all_to_all x4, blocking collectives, exchange(): lax.all_to_all(array, axis, 0, 0, tiled=True, axis_index_groups=members)  41.6 us
    all_gather x1, blocking collectives, body(): both = lax.all_gather(sent, 'col', axis_index_groups=CORES, tiled=True)  8.5 us
    pallas_call x1, Pallas kernels, body(): call(y_join, [(VARS, 8, 16, 128)], [(VARS, 128, 128), (20, 8, 128), (320,...  1.36 us
    pallas_call x1, Pallas kernels, body(): pl.pallas_call(x_local, in_specs=[pl.BlockSpec(memory_space=pltpu.HBM)] *...  1.31 us

profile of v1, /device:TPU:1, one launch (start us, length us, event | category | flops | bytes accessed | tf_op | source)
XLA Modules:
  0.0 54.0 jit_solution(9837386553612546931)
XLA Ops:
  0.0 1.3 %shard_map.37 = (f32[16,9,8,128]{3,2,1,0:T(8,128)S(1)}, f32[320,128]{1,0:T(8,128)S(1)}) custom-call(bf16[5,8,16,128]{3,2,1,0:T(8,128)(2,1)} %right_hbm.1, bf16[3,2,8,16,128]{4,3,2,1,0:T(8,128)(2,1)} %bands_ref.3, bf16[3,8,16,128]{3,2,1,0:T(8,128)(2,1)} %margins_ref.3), custom_call_target="tpu_custom_call" | custom-call | tf_op jit(solution)/shard_map/pallas_call | solution.py:363
  1.3 12.0 %all_to_all.20 = f32[8,40,128]{2,1,0:T(8,128)S(1)} all-to-all(f32[8,40,128]{2,1,0:T(8,128)S(1)} %bitcast.14), channel_id=1, replica_groups={{64,48,80,32,96,16,112,0},{192,176,208,160,224,144,240,128},{320,304,33..., dimensions={0} | all-to-all | bytes 327680 | tf_op jit(solution)/shard_map/all_to_all | solution.py:359
  13.3 0.2 shard_map.38
  13.5 7.7 %all_to_all.21 = f32[4,40,128]{2,1,0:T(8,128)S(1)} all-to-all(f32[4,40,128]{2,1,0:T(8,128)S(1)} %bitcast.15), channel_id=1, replica_groups={{256,128,384,0},{272,144,400,16},{288,160,416,32},{304,176,432,48},{320..., dimensions={0} | all-to-all | bytes 163840 | tf_op jit(solution)/shard_map/all_to_all | solution.py:359
  21.2 0.0 copy-start.1
  21.2 0.3 shard_map.39
  21.4 0.0 copy-start
  21.4 9.3 %all_to_all.22 = f32[8,24,128]{2,1,0:T(8,128)S(1)} all-to-all(f32[8,24,128]{2,1,0:T(8,128)S(1)} %bitcast.10), channel_id=1, replica_groups={{64,48,80,32,96,16,112,0},{192,176,208,160,224,144,240,128},{320,304,33..., dimensions={0} | all-to-all | bytes 196608 | tf_op jit(solution)/shard_map/all_to_all | solution.py:359
  30.7 0.0 copy-done.1
  30.7 0.0 copy-done
  30.8 0.7 %shard_map.40 = (f32[16,9,8,128]{3,2,1,0:T(8,128)S(1)}, f32[3,36,8,128]{3,2,1,0:T(8,128)S(1)}, f32[40,128]{1,0:T(8,128)S(1)}) custom-call(f32[16,9,8,128]{3,2,1,0:T(8,128)S(1)} %get-tuple-element.14.x_solved_ref, f32[192,128]{1,0:T(8,128)S(1)} %bitcast.11, bf16[3,2,8,16,128]{4,3,2,1,0:T(8,128)(2,1)S(1)} %copy-done, bf16[3,8,16,128]{3,2,1,0:T(8,128)(2,1)S(1)} %copy-done.1), custom_call_target="tpu_custom_call" | custom-call | tf_op jit(solution)/shard_map/pallas_call | solution.py:378
  31.5 8.5 %all_gather.3.got_ref = f32[80,128]{1,0:T(8,128)S(1)} all-gather(f32[40,128]{1,0:T(8,128)S(1)} %get-tuple-element.18), channel_id=1, replica_groups={{0,1},{2,3},{4,5},{6,7},{8,9},{10,11},{12,13},{14,15},{16,17},{18,19},{..., dimensions={0}, use_global_device_ids=true | all-gather | bytes 61440 | tf_op jit(solution)/shard_map/all_gather | solution.py:381
  40.0 0.1 shard_map.41
  40.0 12.6 %all_to_all.23 = f32[8,40,128]{2,1,0:T(8,128)S(1)} all-to-all(f32[8,40,128]{2,1,0:T(8,128)S(1)} %bitcast.13), channel_id=1, replica_groups={{12,14,10,8,6,4,2,0},{13,15,11,9,7,5,3,1},{28,30,26,24,22,20,18,16},{29..., dimensions={0} | all-to-all | bytes 327680 | tf_op jit(solution)/shard_map/all_to_all | solution.py:359
  52.6 1.4 %shard_map.42 = f32[5,8,16,128]{3,2,1,0:T(8,128)} custom-call(f32[320,128]{1,0:T(8,128)S(1)} %bitcast.8, f32[36,128]{1,0:T(8,128)S(1)} %get-tuple-element.20.pair_ref, f32[16,9,8,128]{3,2,1,0:T(8,128)S(1)} %get-tuple-element.21.y_solved_ref, f32[3,36,8,128]{3,2,1,0:T(8,128)S(1)} %get-tuple-element.22.kept_ref, bf16[3,2,8,16,128]{4,3,2,1,0:T(8,128)(2,1)S(1)} %copy-done, ...), custom_call_target="tpu_custom_call" | custom-call | tf_op jit(solution)/shard_map/pallas_call | solution.py:383
Async XLA Ops:
  21.2 9.6 %copy-start.1 = (bf16[3,8,16,128]{3,2,1,0:T(8,128)(2,1)S(1)}, bf16[3,8,16,128]{3,2,1,0:T(8,128)(2,1)}, u32[]{:S(2)}) copy-start(bf16[3,8,16,128]{3,2,1,0:T(8,128)(2,1)} %margins_ref.3) | copy-start | bytes 294916
  21.4 9.3 %copy-start = (bf16[3,2,8,16,128]{4,3,2,1,0:T(8,128)(2,1)S(1)}, bf16[3,2,8,16,128]{4,3,2,1,0:T(8,128)(2,1)}, u32[]{:S(2)}) copy-start(bf16[3,2,8,16,128]{4,3,2,1,0:T(8,128)(2,1)} %bands_ref.3) | copy-start | bytes 589828

commit v2 on v1

--- a/solution.py
+++ b/solution.py
@@ -135,30 +135,52 @@
 
 def climb(relation, levels):
     kept = []
-    for axis, distance, size in levels:
-        relation, saved = merge(relation, rolled(relation, size - distance, axis))
+    for axis, distance, size, mirrored in levels:
+        other = rolled(relation, size - distance, axis)
+        relation, saved = merge(other, relation) if mirrored else merge(relation, other)
         kept.append(saved)
     return relation, kept
 
 
 def descend(kept, levels, prev, following):
-    for saved, (axis, distance, size) in zip(reversed(kept), reversed(levels)):
+    for saved, (axis, distance, size, mirrored) in zip(reversed(kept), reversed(levels)):
         tail, head = joint(saved, prev, following)
         place = lax.broadcasted_iota(jnp.int32, (8, 128), axis)
-        is_right = (place & distance) != 0
-        prev = [jnp.where(is_right, pltpu.roll(t, distance, axis), p) for t, p in zip(tail, prev)]
-        following = [jnp.where(is_right, pltpu.roll(f, distance, axis), h) for f, h in zip(following, head)]
+        far = (place & distance) != 0
+        if mirrored:
+            prev = [jnp.where(far, pltpu.roll(p, distance, axis), t) for t, p in zip(tail, prev)]
+            following = [jnp.where(far, pltpu.roll(h, distance, axis), f) for f, h in zip(following, head)]
+        else:
+            prev = [jnp.where(far, pltpu.roll(t, distance, axis), p) for t, p in zip(tail, prev)]
+            following = [jnp.where(far, pltpu.roll(f, distance, axis), h) for f, h in zip(following, head)]
     return prev, following
 
 
-RING_ORDER, ACROSS_ORDER, DEEP_ORDER = (4, 3, 5, 2, 6, 1, 7, 0), (2, 1, 3, 0), (6, 7, 5, 4, 3, 2, 1, 0)
-RING = [[8 * x + y for y in RING_ORDER] for x in range(4)]
-ACROSS = [[8 * x + y for x in ACROSS_ORDER] for y in range(8)]
-DEEP = [[2 * z + core for z in DEEP_ORDER] for core in range(2)]
+def swap_quarters(four):
+    lane = lax.broadcasted_iota(jnp.int32, (8, 128), 1)
+    low_two, low_one = (lane & 64) == 0, (lane & 32) == 0
+    half = [None] * 4
+    for j in (0, 1):
+        a, b = four[j], four[j + 2]
+        half[j] = jnp.where(low_two, a, pltpu.roll(b, 64, 1))
+        half[j + 2] = jnp.where(low_two, pltpu.roll(a, 64, 1), b)
+    out = [None] * 4
+    for j in (0, 2):
+        a, b = half[j], half[j + 1]
+        out[j] = jnp.where(low_one, a, pltpu.roll(b, 32, 1))
+        out[j + 1] = jnp.where(low_one, pltpu.roll(a, 96, 1), b)
+    return out
+
+
+ROW_MASK, DEEP_MASK = 20, 6
+ROWS = [[k ^ ROW_MASK for k in range(32)]]
+DEEP = [[2 * (k ^ DEEP_MASK) + core for k in range(8)] for core in range(2)]
 CORES = [[2 * z, 2 * z + 1] for z in range(8)]
 
-FOUR_LEVELS = ((0, 1, 8), (0, 2, 8))
-SUB_LEVELS = ((0, 1, 8), (0, 2, 8), (0, 4, 8))
+SUB_LEVELS = tuple((0, 1 << bit, 8, False) for bit in range(3))
+DEEP_LEVELS = tuple((0, 1 << bit, 8, bool(DEEP_MASK >> bit & 1)) for bit in range(3))
+ROW_LEVELS = tuple((1, 32 << bit, 128, bool(ROW_MASK >> bit & 1)) for bit in range(2))
+ROW_LEVELS += tuple((0, 1 << bit, 8, bool(ROW_MASK >> bit + 2 & 1)) for bit in range(3))
 
 
 def bands_of(bands_ref, margins_ref, direction):
@@ -195,17 +217,18 @@
         for c in range(VARS + 4):
             solved_ref[i, c] = solved[i][c]
     relation = relation_of(solved)
-    for c in range(36):
-        sent_ref[pl.ds(c, 8, stride=40), :] = relation[c]
+    for g in range(9):
+        out = swap_quarters(relation[4 * g : 4 * g + 4])
+        for quarter in range(4):
+            sent_ref[pl.ds(quarter * 9 + g, 8, stride=36), :] = out[quarter]
 
 
 def send_to_all(relation, sent_ref, row, count):
-    row[...] = jnp.zeros_like(row)
     for c in range(36):
         row[c : c + 1, :] = relation[c][0:1, :]
     whole = row[...]
     for j in range(count):
-        sent_ref[pl.ds(j * 40, 40), :] = whole
+        sent_ref[j * 36 : j * 36 + 36, :] = whole
 
 
 def own_part(values, place, row):
@@ -214,35 +237,18 @@
     return [jnp.broadcast_to(row[c, pl.ds(place, 1), :], (8, 128)) for c in range(len(values))]
 
 
-def in_order(got_ref, ordered, order):
-    for position, member in enumerate(order):
-        ordered[member * 40 : member * 40 + 40, :] = got_ref[position * 40 : position * 40 + 40, :]
-    return [ordered[pl.ds(c, 8, stride=40), :] for c in range(36)]
-
-
-def x_ring(got_ref, kept_ref, sent_ref, row, ordered):
-    relation, kept = climb(in_order(got_ref, ordered, RING_ORDER), SUB_LEVELS)
-    for level in range(3):
-        for c in range(36):
-            kept_ref[level, c] = kept[level][c]
-    send_to_all(relation, sent_ref, row, 4)
-
-
-def x_join(got_ref, kept_ref, sent_ref, twice, row, ordered):
-    for half in range(2):
-        for position, member in enumerate(ACROSS_ORDER):
-            start = half * 160 + member * 40
-            twice[start : start + 40, :] = got_ref[position * 40 : position * 40 + 40, :]
-    _, kept = climb([twice[pl.ds(c, 8, stride=40), :] for c in range(36)], FOUR_LEVELS)
+def x_join(got_ref, sent_ref):
+    relation = []
+    for g in range(9):
+        relation += swap_quarters([got_ref[pl.ds(quarter * 9 + g, 8, stride=36), :] for quarter in range(4)])
+    _, kept = climb(relation, ROW_LEVELS)
     zero = [jnp.zeros((8, 128), F32)] * 10
-    prev, following = descend(kept, FOUR_LEVELS, zero, zero)
-    own = own_part(prev + following, lax.axis_index("row") // 8, row)
-    kept = [[kept_ref[level, c] for c in range(36)] for level in range(3)]
-    prev, following = descend(kept, SUB_LEVELS, own[:10], own[10:])
-    for c, value in enumerate(prev + following):
-        ordered[pl.ds(c, 8, stride=24), :] = value
-    for position, member in enumerate(RING_ORDER):
-        sent_ref[position * 24 : position * 24 + 24, :] = ordered[member * 24 : member * 24 + 24, :]
+    prev, following = descend(kept, ROW_LEVELS, zero, zero)
+    answer = prev + following
+    for g in range(5):
+        out = swap_quarters(answer[4 * g : 4 * g + 4])
+        for quarter in range(4):
+            sent_ref[pl.ds(quarter * 5 + g, 8, stride=20), :] = out[quarter]
 
 
 def with_neighbours(cell, prev, following):
@@ -258,7 +264,9 @@
 
 
 def y_local(x_solved_ref, got_ref, bands_ref, margins_ref, solved_ref, kept_ref, sent_ref, lines, row):
-    answer = [got_ref[pl.ds(c, 8, stride=24), :] for c in range(20)]
+    answer = []
+    for g in range(5):
+        answer += swap_quarters([got_ref[pl.ds(quarter * 5 + g, 8, stride=20), :] for quarter in range(4)])
     prev, following = answer[:10], answer[10:]
     for i in range(16):
         cell = [x_solved_ref[i, c] for c in range(VARS + 4)]
@@ -285,19 +293,19 @@
 
 
 def y_pair(got_ref, pair_ref, sent_ref, row):
-    left, right = ([got_ref[40 * s + c : 40 * s + c + 1, :] for c in range(36)] for s in range(2))
+    left, right = ([got_ref[36 * s + c : 36 * s + c + 1, :] for c in range(36)] for s in range(2))
     relation, pair = merge(left, right)
     for c in range(36):
         pair_ref[c : c + 1, :] = pair[c]
     send_to_all(relation, sent_ref, row, 8)
 
 
-def y_join(got_ref, pair_ref, y_solved_ref, kept_ref, bands_ref, margins_ref, out_ref, lines, row, ordered):
+def y_join(got_ref, pair_ref, y_solved_ref, kept_ref, bands_ref, margins_ref, out_ref, lines, row):
     mine = lax.axis_index("col")
-    _, kept = climb(in_order(got_ref, ordered, DEEP_ORDER), SUB_LEVELS)
+    _, kept = climb([got_ref[pl.ds(c, 8, stride=36), :] for c in range(36)], DEEP_LEVELS)
     zero = [jnp.zeros((8, 128), F32)] * 10
-    prev, following = descend(kept, SUB_LEVELS, zero, zero)
-    own = own_part(prev + following, mine // 2, row)
+    prev, following = descend(kept, DEEP_LEVELS, zero, zero)
+    own = own_part(prev + following, (mine // 2) ^ DEEP_MASK, row)
     prev, following = own[:10], own[10:]
     tail, head = joint([pair_ref[c : c + 1, :] for c in range(36)], prev, following)
     is_right = jnp.full((8, 128), mine % 2, jnp.int32) != 0
@@ -354,8 +362,8 @@
     )
 
 
-def exchange(array, axis, count, members=None):
-    array = array.reshape(count, -1, 128)
+def exchange(array, axis, members, rows):
+    array = array.reshape(len(members[0]), -1, rows, 128)
     return lax.all_to_all(array, axis, 0, 0, tiled=True, axis_index_groups=members).reshape(-1, 128)
 
 
@@ -363,7 +371,7 @@
     x_solved, sent = pl.pallas_call(
         x_local,
         in_specs=[pl.BlockSpec(memory_space=pltpu.HBM)] * 3,
-        out_shape=[jax.ShapeDtypeStruct((16, 9, 8, 128), F32), jax.ShapeDtypeStruct((320, 128), F32)],
+        out_shape=[jax.ShapeDtypeStruct((16, 9, 8, 128), F32), jax.ShapeDtypeStruct((288, 128), F32)],
         scratch_shapes=[
             pltpu.VMEM((8, 128, 128), F32),
             pltpu.VMEM((VARS, 8, 16, 128), jnp.bfloat16),
@@ -373,15 +381,14 @@
         ],
         compiler_params=PARAMS,
     )(*[pltpu.with_memory_space_constraint(a, pltpu.HBM) for a in (right_side, near_bands, margins)])
-    kept, sent = call(x_ring, [(3, 36, 8, 128), (160, 128)], [(40, 128), (320, 128)])(exchange(sent, "row", 8, RING))
-    (answer,) = call(x_join, [(192, 128)], [(320, 128), (20, 8, 128), (192, 128)])(exchange(sent, "row", 4, ACROSS), kept)
+    (answer,) = call(x_join, [(160, 128)], [])(exchange(sent, "row", ROWS, 1))
     y_solved, kept, sent = call(
-        y_local, [(16, 9, 8, 128), (3, 36, 8, 128), (40, 128)], [(8, 128, 128), (40, 128)]
-    )(x_solved, exchange(answer, "row", 8, RING), near_bands, margins)
+        y_local, [(16, 9, 8, 128), (3, 36, 8, 128), (36, 128)], [(8, 128, 128), (36, 128)]
+    )(x_solved, exchange(answer, "row", ROWS, 1), near_bands, margins)
     both = lax.all_gather(sent, "col", axis_index_groups=CORES, tiled=True)
-    pair, sent = call(y_pair, [(36, 128), (320, 128)], [(40, 128)])(both)
-    (update,) = call(y_join, [(VARS, 8, 16, 128)], [(VARS, 128, 128), (20, 8, 128), (320, 128)])(
-        exchange(sent, "col", 8, DEEP), pair, y_solved, kept, near_bands, margins
+    pair, sent = call(y_pair, [(36, 128), (288, 128)], [(36, 128)])(both)
+    (update,) = call(y_join, [(VARS, 8, 16, 128)], [(VARS, 128, 128), (20, 8, 128)])(
+        exchange(sent, "col", DEEP, 4), pair, y_solved, kept, near_bands, margins
     )
     return update
 

time: 54.8 us -> 52.5 us (0.958)
  blocking collectives: 50.1 us -> 47.2 us
  Pallas kernels: 3.91 us -> 4.51 us
    all_to_all x4 -> x3, blocking collectives: 41.6 us -> 38.6 us  [exchange(): lax.all_to_all(array, axis, 0, 0, tiled=True, axis_index_groups=members)]
    pallas_call x5 -> x4, Pallas kernels: 2.6 us -> 3.04 us  [the longest x1 1.32 us: body(): call(y_join, [(VARS, 8, 16, 128)], [(VARS, 128, 128), (20, 8, 128)])]
where the time goes in v2:
time: 52.5 us; the launch traced here: 51.8 us
  blocking collectives  47.2 us (90%)
  Pallas kernels  4.51 us (9%)
    all_to_all x3, blocking collectives, exchange(): lax.all_to_all(array, axis, 0, 0, tiled=True, axis_index_groups=members)  38.6 us
    all_gather x1, blocking collectives, body(): both = lax.all_gather(sent, 'col', axis_index_groups=CORES, tiled=True)  8.66 us
    pallas_call x1, Pallas kernels, body(): pl.pallas_call(x_local, in_specs=[pl.BlockSpec(memory_space=pltpu.HBM)] *...  1.47 us
    pallas_call x1, Pallas kernels, body(): call(y_join, [(VARS, 8, 16, 128)], [(VARS, 128, 128), (20, 8, 128)])  1.32 us

profile of v2, /device:TPU:1, one launch (start us, length us, event | category | flops | bytes accessed | tf_op | source)
XLA Modules:
  0.0 51.8 jit_solution(13757869251609528113)
XLA Ops:
  0.0 1.5 %shard_map.37 = (f32[16,9,8,128]{3,2,1,0:T(8,128)S(1)}, f32[288,128]{1,0:T(8,128)S(1)}) custom-call(bf16[5,8,16,128]{3,2,1,0:T(8,128)(2,1)} %right_hbm.1, bf16[3,2,8,16,128]{4,3,2,1,0:T(8,128)(2,1)} %bands_ref.3, bf16[3,8,16,128]{3,2,1,0:T(8,128)(2,1)} %margins_ref.3), custom_call_target="tpu_custom_call" | custom-call | tf_op jit(solution)/shard_map/pallas_call | solution.py:371
  1.5 14.3 %all_to_all.15 = f32[32,9,1,128]{3,2,1,0:T(1,128)S(1)} all-to-all(f32[32,9,1,128]{3,2,1,0:T(1,128)S(1)} %bitcast.12), channel_id=1, replica_groups={{320,336,352,368,256,272,288,304,448,464,480,496,384,400,416,432,64,80,..., dimensions={0} | all-to-all | bytes 294912 | tf_op jit(solution)/shard_map/all_to_all | solution.py:367
  15.8 0.0 copy-start
  15.8 0.9 %shard_map.38 = f32[160,128]{1,0:T(8,128)S(1)} custom-call(f32[288,128]{1,0:T(8,128)S(1)} %bitcast.8), custom_call_target="tpu_custom_call" | custom-call | tf_op jit(solution)/shard_map/pallas_call | solution.py:384
  16.7 0.0 copy-start.1
  16.7 12.1 %all_to_all.16 = f32[32,5,1,128]{3,2,1,0:T(1,128)S(1)} all-to-all(f32[32,5,1,128]{3,2,1,0:T(1,128)S(1)} %bitcast.9), channel_id=1, replica_groups={{320,336,352,368,256,272,288,304,448,464,480,496,384,400,416,432,64,80,..., dimensions={0} | all-to-all | bytes 163840 | tf_op jit(solution)/shard_map/all_to_all | solution.py:367
  28.8 0.0 copy-done
  28.8 0.0 copy-done.1
  28.8 0.8 %shard_map.39 = (f32[16,9,8,128]{3,2,1,0:T(8,128)S(1)}, f32[3,36,8,128]{3,2,1,0:T(8,128)S(1)}, f32[36,128]{1,0:T(8,128)S(1)}) custom-call(f32[16,9,8,128]{3,2,1,0:T(8,128)S(1)} %get-tuple-element.12.x_solved_ref, f32[160,128]{1,0:T(8,128)S(1)} %bitcast.10, bf16[3,2,8,16,128]{4,3,2,1,0:T(8,128)(2,1)S(1)} %copy-done, bf16[3,8,16,128]{3,2,1,0:T(8,128)(2,1)S(1)} %copy-done.1), custom_call_target="tpu_custom_call" | custom-call | tf_op jit(solution)/shard_map/pallas_call | solution.py:385
  29.6 8.7 %all-gather = f32[2,36,128]{2,1,0:T(8,128)S(1)} all-gather(f32[1,36,128]{2,1,0:T(8,128)S(1)} %bitcast.13), channel_id=1, replica_groups={{0,1},{2,3},{4,5},{6,7},{8,9},{10,11},{12,13},{14,15},{16,17},{18,19},{..., dimensions={0}, use_global_device_ids=true | all-gather | bytes 55296 | tf_op jit(solution)/shard_map/all_gather | solution.py:388
  38.3 0.1 shard_map.40
  38.3 12.1 %all_to_all.17 = f32[8,9,4,128]{3,2,1,0:T(4,128)S(1)} all-to-all(f32[8,9,4,128]{3,2,1,0:T(4,128)S(1)} %bitcast.11), channel_id=1, replica_groups={{12,14,8,10,4,6,0,2},{13,15,9,11,5,7,1,3},{28,30,24,26,20,22,16,18},{29..., dimensions={0} | all-to-all | bytes 294912 | tf_op jit(solution)/shard_map/all_to_all | solution.py:367
  50.5 1.3 %shard_map.41 = f32[5,8,16,128]{3,2,1,0:T(8,128)} custom-call(f32[288,128]{1,0:T(8,128)S(1)} %bitcast.7, f32[36,128]{1,0:T(8,128)S(1)} %get-tuple-element.16.pair_ref, f32[16,9,8,128]{3,2,1,0:T(8,128)S(1)} %get-tuple-element.17.y_solved_ref, f32[3,36,8,128]{3,2,1,0:T(8,128)S(1)} %get-tuple-element.18.kept_ref, bf16[3,2,8,16,128]{4,3,2,1,0:T(8,128)(2,1)S(1)} %copy-done, ...), custom_call_target="tpu_custom_call" | custom-call | tf_op jit(solution)/shard_map/pallas_call | solution.py:390
  (1 shorter events, 0.0 us)
Async XLA Ops:
  15.8 13.0 %copy-start = (bf16[3,2,8,16,128]{4,3,2,1,0:T(8,128)(2,1)S(1)}, bf16[3,2,8,16,128]{4,3,2,1,0:T(8,128)(2,1)}, u32[]{:S(2)}) copy-start(bf16[3,2,8,16,128]{4,3,2,1,0:T(8,128)(2,1)} %bands_ref.3) | copy-start | bytes 589828
  16.7 12.1 %copy-start.1 = (bf16[3,8,16,128]{3,2,1,0:T(8,128)(2,1)S(1)}, bf16[3,8,16,128]{3,2,1,0:T(8,128)(2,1)}, u32[]{:S(2)}) copy-start(bf16[3,8,16,128]{3,2,1,0:T(8,128)(2,1)} %margins_ref.3) | copy-start | bytes 294916

commit v3 on v2

--- a/solution.py
+++ b/solution.py
@@ -124,6 +124,8 @@
 
 def joint(saved, prev, following):
     jv, kv, jp, jf, kp, kf = saved[:10], saved[10:20], saved[20:24], saved[24:28], saved[28:32], saved[32:]
+    if prev is None:
+        return jv, kv
     tail = plus(minus(jv, product(jp, prev)), product(jf, following))
     head = minus(plus(kv, product(kp, prev)), product(kf, following))
     return tail, head
@@ -147,6 +149,8 @@
         tail, head = joint(saved, prev, following)
         place = lax.broadcasted_iota(jnp.int32, (8, 128), axis)
         far = (place & distance) != 0
+        if prev is None:
+            prev = following = [jnp.zeros((8, 128), F32)] * 10
         if mirrored:
             prev = [jnp.where(far, pltpu.roll(p, distance, axis), t) for t, p in zip(tail, prev)]
             following = [jnp.where(far, pltpu.roll(h, distance, axis), f) for f, h in zip(following, head)]
@@ -172,13 +176,12 @@
     return out
 
 
-ROW_MASK, DEEP_MASK = 20, 6
+ROW_MASK, DEEP_ORDER = 20, (6, 7, 5, 4, 3, 2, 1, 0)
 ROWS = [[k ^ ROW_MASK for k in range(32)]]
-DEEP = [[2 * (k ^ DEEP_MASK) + core for k in range(8)] for core in range(2)]
+DEEP = [[2 * z + core for z in DEEP_ORDER] for core in range(2)]
 CORES = [[2 * z, 2 * z + 1] for z in range(8)]
 
 SUB_LEVELS = tuple((0, 1 << bit, 8, False) for bit in range(3))
-DEEP_LEVELS = tuple((0, 1 << bit, 8, bool(DEEP_MASK >> bit & 1)) for bit in range(3))
 ROW_LEVELS = tuple((1, 32 << bit, 128, bool(ROW_MASK >> bit & 1)) for bit in range(2))
 ROW_LEVELS += tuple((0, 1 << bit, 8, bool(ROW_MASK >> bit + 2 & 1)) for bit in range(3))
 
@@ -242,8 +245,7 @@
     for g in range(9):
         relation += swap_quarters([got_ref[pl.ds(quarter * 9 + g, 8, stride=36), :] for quarter in range(4)])
     _, kept = climb(relation, ROW_LEVELS)
-    zero = [jnp.zeros((8, 128), F32)] * 10
-    prev, following = descend(kept, ROW_LEVELS, zero, zero)
+    prev, following = descend(kept, ROW_LEVELS, None, None)
     answer = prev + following
     for g in range(5):
         out = swap_quarters(answer[4 * g : 4 * g + 4])
@@ -300,12 +302,13 @@
     send_to_all(relation, sent_ref, row, 8)
 
 
-def y_join(got_ref, pair_ref, y_solved_ref, kept_ref, bands_ref, margins_ref, out_ref, lines, row):
+def y_join(got_ref, pair_ref, y_solved_ref, kept_ref, bands_ref, margins_ref, out_ref, lines, row, ordered):
     mine = lax.axis_index("col")
-    _, kept = climb([got_ref[pl.ds(c, 8, stride=36), :] for c in range(36)], DEEP_LEVELS)
-    zero = [jnp.zeros((8, 128), F32)] * 10
-    prev, following = descend(kept, DEEP_LEVELS, zero, zero)
-    own = own_part(prev + following, (mine // 2) ^ DEEP_MASK, row)
+    for position, z in enumerate(DEEP_ORDER):
+        ordered[z * 40 : z * 40 + 36, :] = got_ref[position * 36 : position * 36 + 36, :]
+    _, kept = climb([ordered[pl.ds(c, 8, stride=40), :] for c in range(36)], SUB_LEVELS)
+    prev, following = descend(kept, SUB_LEVELS, None, None)
+    own = own_part(prev + following, mine // 2, row)
     prev, following = own[:10], own[10:]
     tail, head = joint([pair_ref[c : c + 1, :] for c in range(36)], prev, following)
     is_right = jnp.full((8, 128), mine % 2, jnp.int32) != 0
@@ -387,7 +390,7 @@
     )(x_solved, exchange(answer, "row", ROWS, 1), near_bands, margins)
     both = lax.all_gather(sent, "col", axis_index_groups=CORES, tiled=True)
     pair, sent = call(y_pair, [(36, 128), (288, 128)], [(36, 128)])(both)
-    (update,) = call(y_join, [(VARS, 8, 16, 128)], [(VARS, 128, 128), (20, 8, 128)])(
+    (update,) = call(y_join, [(VARS, 8, 16, 128)], [(VARS, 128, 128), (20, 8, 128), (320, 128)])(
         exchange(sent, "col", DEEP, 4), pair, y_solved, kept, near_bands, margins
     )
     return update

time: 52.5 us -> 51.9 us (0.989)
  no operation moved by 1% of the time
where the time goes in v3:
time: 51.9 us; the launch traced here: 51.4 us
  blocking collectives  46.9 us (90%)
  Pallas kernels  4.49 us (9%)
    all_to_all x3, blocking collectives, exchange(): lax.all_to_all(array, axis, 0, 0, tiled=True, axis_index_groups=members)  38.2 us
    all_gather x1, blocking collectives, body(): both = lax.all_gather(sent, 'col', axis_index_groups=CORES, tiled=True)  8.66 us
    pallas_call x1, Pallas kernels, body(): pl.pallas_call(x_local, in_specs=[pl.BlockSpec(memory_space=pltpu.HBM)] *...  1.47 us
    pallas_call x1, Pallas kernels, body(): call(y_join, [(VARS, 8, 16, 128)], [(VARS, 128, 128), (20, 8, 128), (320,...  1.33 us

profile of v3, /device:TPU:1, one launch (start us, length us, event | category | flops | bytes accessed | tf_op | source)
XLA Modules:
  0.0 51.4 jit_solution(3317644612509672162)
XLA Ops:
  0.0 1.5 %shard_map.37 = (f32[16,9,8,128]{3,2,1,0:T(8,128)S(1)}, f32[288,128]{1,0:T(8,128)S(1)}) custom-call(bf16[5,8,16,128]{3,2,1,0:T(8,128)(2,1)} %right_hbm.1, bf16[3,2,8,16,128]{4,3,2,1,0:T(8,128)(2,1)} %bands_ref.3, bf16[3,8,16,128]{3,2,1,0:T(8,128)(2,1)} %margins_ref.3), custom_call_target="tpu_custom_call" | custom-call | tf_op jit(solution)/shard_map/pallas_call | solution.py:374
  1.5 14.3 %all_to_all.15 = f32[32,9,1,128]{3,2,1,0:T(1,128)S(1)} all-to-all(f32[32,9,1,128]{3,2,1,0:T(1,128)S(1)} %bitcast.12), channel_id=1, replica_groups={{320,336,352,368,256,272,288,304,448,464,480,496,384,400,416,432,64,80,..., dimensions={0} | all-to-all | bytes 294912 | tf_op jit(solution)/shard_map/all_to_all | solution.py:370
  15.8 0.0 copy-start
  15.8 0.9 %shard_map.38 = f32[160,128]{1,0:T(8,128)S(1)} custom-call(f32[288,128]{1,0:T(8,128)S(1)} %bitcast.8), custom_call_target="tpu_custom_call" | custom-call | tf_op jit(solution)/shard_map/pallas_call | solution.py:387
  16.7 0.0 copy-start.1
  16.7 12.1 %all_to_all.16 = f32[32,5,1,128]{3,2,1,0:T(1,128)S(1)} all-to-all(f32[32,5,1,128]{3,2,1,0:T(1,128)S(1)} %bitcast.9), channel_id=1, replica_groups={{320,336,352,368,256,272,288,304,448,464,480,496,384,400,416,432,64,80,..., dimensions={0} | all-to-all | bytes 163840 | tf_op jit(solution)/shard_map/all_to_all | solution.py:370
  28.8 0.0 copy-done
  28.8 0.0 copy-done.1
  28.8 0.8 %shard_map.39 = (f32[16,9,8,128]{3,2,1,0:T(8,128)S(1)}, f32[3,36,8,128]{3,2,1,0:T(8,128)S(1)}, f32[36,128]{1,0:T(8,128)S(1)}) custom-call(f32[16,9,8,128]{3,2,1,0:T(8,128)S(1)} %get-tuple-element.12.x_solved_ref, f32[160,128]{1,0:T(8,128)S(1)} %bitcast.10, bf16[3,2,8,16,128]{4,3,2,1,0:T(8,128)(2,1)S(1)} %copy-done, bf16[3,8,16,128]{3,2,1,0:T(8,128)(2,1)S(1)} %copy-done.1), custom_call_target="tpu_custom_call" | custom-call | tf_op jit(solution)/shard_map/pallas_call | solution.py:388
  29.6 8.7 %all-gather = f32[2,36,128]{2,1,0:T(8,128)S(1)} all-gather(f32[1,36,128]{2,1,0:T(8,128)S(1)} %bitcast.13), channel_id=1, replica_groups={{0,1},{2,3},{4,5},{6,7},{8,9},{10,11},{12,13},{14,15},{16,17},{18,19},{..., dimensions={0}, use_global_device_ids=true | all-gather | bytes 55296 | tf_op jit(solution)/shard_map/all_gather | solution.py:391
  38.2 0.1 shard_map.40
  38.3 11.8 %all_to_all.17 = f32[8,9,4,128]{3,2,1,0:T(4,128)S(1)} all-to-all(f32[8,9,4,128]{3,2,1,0:T(4,128)S(1)} %bitcast.11), channel_id=1, replica_groups={{12,14,10,8,6,4,2,0},{13,15,11,9,7,5,3,1},{28,30,26,24,22,20,18,16},{29..., dimensions={0} | all-to-all | bytes 294912 | tf_op jit(solution)/shard_map/all_to_all | solution.py:370
  50.1 1.3 %shard_map.41 = f32[5,8,16,128]{3,2,1,0:T(8,128)} custom-call(f32[288,128]{1,0:T(8,128)S(1)} %bitcast.7, f32[36,128]{1,0:T(8,128)S(1)} %get-tuple-element.16.pair_ref, f32[16,9,8,128]{3,2,1,0:T(8,128)S(1)} %get-tuple-element.17.y_solved_ref, f32[3,36,8,128]{3,2,1,0:T(8,128)S(1)} %get-tuple-element.18.kept_ref, bf16[3,2,8,16,128]{4,3,2,1,0:T(8,128)(2,1)S(1)} %copy-done, ...), custom_call_target="tpu_custom_call" | custom-call | tf_op jit(solution)/shard_map/pallas_call | solution.py:393
  (1 shorter events, 0.0 us)
Async XLA Ops:
  15.8 13.0 %copy-start = (bf16[3,2,8,16,128]{4,3,2,1,0:T(8,128)(2,1)S(1)}, bf16[3,2,8,16,128]{4,3,2,1,0:T(8,128)(2,1)}, u32[]{:S(2)}) copy-start(bf16[3,2,8,16,128]{4,3,2,1,0:T(8,128)(2,1)} %bands_ref.3) | copy-start | bytes 589828
  16.7 12.1 %copy-start.1 = (bf16[3,8,16,128]{3,2,1,0:T(8,128)(2,1)S(1)}, bf16[3,8,16,128]{3,2,1,0:T(8,128)(2,1)}, u32[]{:S(2)}) copy-start(bf16[3,8,16,128]{3,2,1,0:T(8,128)(2,1)} %margins_ref.3) | copy-start | bytes 294916

commit v4 on v3

--- a/solution.py
+++ b/solution.py
@@ -7,6 +7,7 @@
 
 VARS = 5
 OUTER = 0.05
+PITCH = 24
 F32 = jnp.float32
 PARAMS = pltpu.CompilerParams(vmem_limit_bytes=48 * 1024 * 1024)
 
@@ -193,29 +194,41 @@
     return below, middle, above
 
 
+def put_pitched(lines, slot, array):
+    for s in range(8):
+        lines[slot, s * PITCH : s * PITCH + 16, :] = array[16 * s : 16 * s + 16, :]
+
+
+def get_pitched(lines, slot):
+    return jnp.concatenate([lines[slot, s * PITCH : s * PITCH + 16, :] for s in range(8)], axis=0)
+
+
+def solve_pitched(lines):
+    def cell(slot):
+        return lambda i: lines[slot, pl.ds(i, 8, stride=PITCH), :]
+
+    sources = [[cell(3 + v)(i) for v in range(VARS)] for i in range(16)]
+    return solve_block(cell(0), cell(1), cell(2), sources, 16)
+
+
 def x_local(right_hbm, bands_hbm, margins_hbm, solved_ref, sent_ref, lines, right, bands, margins, arrived):
     copies = [
-        pltpu.make_async_copy(bands_hbm.at[0], bands, arrived.at[0]),
-        pltpu.make_async_copy(margins_hbm.at[0], margins, arrived.at[1]),
-        pltpu.make_async_copy(right_hbm, right, arrived.at[2]),
+        pltpu.make_async_copy(right_hbm, right, arrived.at[0]),
+        pltpu.make_async_copy(bands_hbm.at[0], bands, arrived.at[1]),
+        pltpu.make_async_copy(margins_hbm.at[0], margins, arrived.at[2]),
     ]
     for copy in copies:
         copy.start()
-    copies[0].wait()
     copies[1].wait()
+    copies[2].wait()
     below, above = bands[0].astype(F32), bands[1].astype(F32)
     middle = jnp.abs(below) + jnp.abs(above) + 0.1 + margins[...].astype(F32)
     for slot, array in enumerate((below, middle, above)):
-        lines[slot] = array.reshape(128, 128)
-    copies[2].wait()
+        put_pitched(lines, slot, array.reshape(128, 128))
+    copies[0].wait()
     for v in range(VARS):
-        lines[3 + v] = right[v].astype(F32).reshape(128, 128)
-
-    def cell(slot):
-        return lambda i: lines[slot, pl.ds(i, 8, stride=16), :]
-
-    sources = [[cell(3 + v)(i) for v in range(VARS)] for i in range(16)]
-    solved = solve_block(cell(0), cell(1), cell(2), sources, 16)
+        put_pitched(lines, 3 + v, right[v].astype(F32).reshape(128, 128))
+    solved = solve_pitched(lines)
     for i in range(16):
         for c in range(VARS + 4):
             solved_ref[i, c] = solved[i][c]
@@ -273,17 +286,12 @@
     for i in range(16):
         cell = [x_solved_ref[i, c] for c in range(VARS + 4)]
         for v, value in enumerate(with_neighbours(cell, prev, following)):
-            lines[3 + v, pl.ds(i, 8, stride=16), :] = value
+            lines[3 + v, pl.ds(i, 8, stride=PITCH), :] = value
     for slot, array in enumerate(bands_of(bands_ref, margins_ref, 1)):
-        lines[slot] = array.reshape(128, 128).T
+        put_pitched(lines, slot, array.reshape(128, 128).T)
     for v in range(VARS):
-        lines[3 + v] = lines[3 + v].T
-
-    def cell_of(slot):
-        return lambda i: lines[slot, pl.ds(i, 8, stride=16), :]
-
-    sources = [[cell_of(3 + v)(i) for v in range(VARS)] for i in range(16)]
-    solved = solve_block(cell_of(0), cell_of(1), cell_of(2), sources, 16)
+        put_pitched(lines, 3 + v, get_pitched(lines, 3 + v).T)
+    solved = solve_pitched(lines)
     for i in range(16):
         for c in range(VARS + 4):
             solved_ref[i, c] = solved[i][c]
@@ -319,10 +327,10 @@
     for i in range(16):
         cell = [y_solved_ref[i, c] for c in range(VARS + 4)]
         for v, value in enumerate(with_neighbours(cell, prev, following)):
-            lines[v, pl.ds(i, 8, stride=16), :] = value
+            lines[v, pl.ds(i, 8, stride=PITCH), :] = value
     below, middle, above = bands_of(bands_ref, margins_ref, 2)
     ratio_one, ratio_two, reduced = [], [], []
-    fields = [lines[v].T.reshape(8, 16, 128) for v in range(VARS)]
+    fields = [get_pitched(lines, v).T.reshape(8, 16, 128) for v in range(VARS)]
     for i in range(8):
         lower = below[i] + OUTER * ratio_one[i - 2] if i >= 2 else below[i]
         centre = middle[i] + OUTER * ratio_two[i - 2] if i >= 2 else middle[i]
@@ -376,7 +384,7 @@
         in_specs=[pl.BlockSpec(memory_space=pltpu.HBM)] * 3,
         out_shape=[jax.ShapeDtypeStruct((16, 9, 8, 128), F32), jax.ShapeDtypeStruct((288, 128), F32)],
         scratch_shapes=[
-            pltpu.VMEM((8, 128, 128), F32),
+            pltpu.VMEM((8, 8 * PITCH, 128), F32),
             pltpu.VMEM((VARS, 8, 16, 128), jnp.bfloat16),
             pltpu.VMEM((2, 8, 16, 128), jnp.bfloat16),
             pltpu.VMEM((8, 16, 128), jnp.bfloat16),
@@ -386,11 +394,11 @@
     )(*[pltpu.with_memory_space_constraint(a, pltpu.HBM) for a in (right_side, near_bands, margins)])
     (answer,) = call(x_join, [(160, 128)], [])(exchange(sent, "row", ROWS, 1))
     y_solved, kept, sent = call(
-        y_local, [(16, 9, 8, 128), (3, 36, 8, 128), (36, 128)], [(8, 128, 128), (36, 128)]
+        y_local, [(16, 9, 8, 128), (3, 36, 8, 128), (36, 128)], [(8, 8 * PITCH, 128), (36, 128)]
     )(x_solved, exchange(answer, "row", ROWS, 1), near_bands, margins)
     both = lax.all_gather(sent, "col", axis_index_groups=CORES, tiled=True)
     pair, sent = call(y_pair, [(36, 128), (288, 128)], [(36, 128)])(both)
-    (update,) = call(y_join, [(VARS, 8, 16, 128)], [(VARS, 128, 128), (20, 8, 128), (320, 128)])(
+    (update,) = call(y_join, [(VARS, 8, 16, 128)], [(VARS, 8 * PITCH, 128), (20, 8, 128), (320, 128)])(
         exchange(sent, "col", DEEP, 4), pair, y_solved, kept, near_bands, margins
     )
     return update

time: 51.9 us -> 51.7 us (level)
  no operation moved by 1% of the time
where the time goes in v4:
time: 51.7 us; the launch traced here: 51.2 us
  blocking collectives  46.9 us (91%)
  Pallas kernels  4.31 us (8%)
    all_to_all x3, blocking collectives, exchange(): lax.all_to_all(array, axis, 0, 0, tiled=True, axis_index_groups=members)  38.2 us
    all_gather x1, blocking collectives, body(): both = lax.all_gather(sent, 'col', axis_index_groups=CORES, tiled=True)  8.66 us
    pallas_call x1, Pallas kernels, body(): pl.pallas_call(x_local, in_specs=[pl.BlockSpec(memory_space=pltpu.HBM)] *...  1.38 us
    pallas_call x1, Pallas kernels, body(): call(y_join, [(VARS, 8, 16, 128)], [(VARS, 8 * PITCH, 128), (20, 8, 128),...  1.31 us

profile of v4, /device:TPU:1, one launch (start us, length us, event | category | flops | bytes accessed | tf_op | source)
XLA Modules:
  0.0 51.2 jit_solution(8406965615083284977)
XLA Ops:
  0.0 1.4 %shard_map.37 = (f32[16,9,8,128]{3,2,1,0:T(8,128)S(1)}, f32[288,128]{1,0:T(8,128)S(1)}) custom-call(bf16[5,8,16,128]{3,2,1,0:T(8,128)(2,1)} %right_hbm.1, bf16[3,2,8,16,128]{4,3,2,1,0:T(8,128)(2,1)} %bands_ref.3, bf16[3,8,16,128]{3,2,1,0:T(8,128)(2,1)} %margins_ref.3), custom_call_target="tpu_custom_call" | custom-call | tf_op jit(solution)/shard_map/pallas_call | solution.py:382
  1.4 14.3 %all_to_all.15 = f32[32,9,1,128]{3,2,1,0:T(1,128)S(1)} all-to-all(f32[32,9,1,128]{3,2,1,0:T(1,128)S(1)} %bitcast.12), channel_id=1, replica_groups={{320,336,352,368,256,272,288,304,448,464,480,496,384,400,416,432,64,80,..., dimensions={0} | all-to-all | bytes 294912 | tf_op jit(solution)/shard_map/all_to_all | solution.py:378
  15.7 0.0 copy-start
  15.7 0.9 %shard_map.38 = f32[160,128]{1,0:T(8,128)S(1)} custom-call(f32[288,128]{1,0:T(8,128)S(1)} %bitcast.8), custom_call_target="tpu_custom_call" | custom-call | tf_op jit(solution)/shard_map/pallas_call | solution.py:395
  16.6 0.0 copy-start.1
  16.6 12.1 %all_to_all.16 = f32[32,5,1,128]{3,2,1,0:T(1,128)S(1)} all-to-all(f32[32,5,1,128]{3,2,1,0:T(1,128)S(1)} %bitcast.9), channel_id=1, replica_groups={{320,336,352,368,256,272,288,304,448,464,480,496,384,400,416,432,64,80,..., dimensions={0} | all-to-all | bytes 163840 | tf_op jit(solution)/shard_map/all_to_all | solution.py:378
  28.7 0.0 copy-done
  28.7 0.0 copy-done.1
  28.7 0.7 %shard_map.39 = (f32[16,9,8,128]{3,2,1,0:T(8,128)S(1)}, f32[3,36,8,128]{3,2,1,0:T(8,128)S(1)}, f32[36,128]{1,0:T(8,128)S(1)}) custom-call(f32[16,9,8,128]{3,2,1,0:T(8,128)S(1)} %get-tuple-element.12.x_solved_ref, f32[160,128]{1,0:T(8,128)S(1)} %bitcast.10, bf16[3,2,8,16,128]{4,3,2,1,0:T(8,128)(2,1)S(1)} %copy-done, bf16[3,8,16,128]{3,2,1,0:T(8,128)(2,1)S(1)} %copy-done.1), custom_call_target="tpu_custom_call" | custom-call | tf_op jit(solution)/shard_map/pallas_call | solution.py:396
  29.4 8.7 %all-gather = f32[2,36,128]{2,1,0:T(8,128)S(1)} all-gather(f32[1,36,128]{2,1,0:T(8,128)S(1)} %bitcast.13), channel_id=1, replica_groups={{0,1},{2,3},{4,5},{6,7},{8,9},{10,11},{12,13},{14,15},{16,17},{18,19},{..., dimensions={0}, use_global_device_ids=true | all-gather | bytes 55296 | tf_op jit(solution)/shard_map/all_gather | solution.py:399
  38.1 0.1 shard_map.40
  38.1 11.8 %all_to_all.17 = f32[8,9,4,128]{3,2,1,0:T(4,128)S(1)} all-to-all(f32[8,9,4,128]{3,2,1,0:T(4,128)S(1)} %bitcast.11), channel_id=1, replica_groups={{12,14,10,8,6,4,2,0},{13,15,11,9,7,5,3,1},{28,30,26,24,22,20,18,16},{29..., dimensions={0} | all-to-all | bytes 294912 | tf_op jit(solution)/shard_map/all_to_all | solution.py:378
  49.9 1.3 %shard_map.41 = f32[5,8,16,128]{3,2,1,0:T(8,128)} custom-call(f32[288,128]{1,0:T(8,128)S(1)} %bitcast.7, f32[36,128]{1,0:T(8,128)S(1)} %get-tuple-element.16.pair_ref, f32[16,9,8,128]{3,2,1,0:T(8,128)S(1)} %get-tuple-element.17.y_solved_ref, f32[3,36,8,128]{3,2,1,0:T(8,128)S(1)} %get-tuple-element.18.kept_ref, bf16[3,2,8,16,128]{4,3,2,1,0:T(8,128)(2,1)S(1)} %copy-done, ...), custom_call_target="tpu_custom_call" | custom-call | tf_op jit(solution)/shard_map/pallas_call | solution.py:401
  (1 shorter events, 0.0 us)
Async XLA Ops:
  15.7 13.0 %copy-start = (bf16[3,2,8,16,128]{4,3,2,1,0:T(8,128)(2,1)S(1)}, bf16[3,2,8,16,128]{4,3,2,1,0:T(8,128)(2,1)}, u32[]{:S(2)}) copy-start(bf16[3,2,8,16,128]{4,3,2,1,0:T(8,128)(2,1)} %bands_ref.3) | copy-start | bytes 589828
  16.6 12.1 %copy-start.1 = (bf16[3,8,16,128]{3,2,1,0:T(8,128)(2,1)S(1)}, bf16[3,8,16,128]{3,2,1,0:T(8,128)(2,1)}, u32[]{:S(2)}) copy-start(bf16[3,8,16,128]{3,2,1,0:T(8,128)(2,1)} %margins_ref.3) | copy-start | bytes 294916

commit v5 on v4

--- a/solution.py
+++ b/solution.py
@@ -213,19 +213,21 @@
 
 def x_local(right_hbm, bands_hbm, margins_hbm, solved_ref, sent_ref, lines, right, bands, margins, arrived):
     copies = [
-        pltpu.make_async_copy(right_hbm, right, arrived.at[0]),
-        pltpu.make_async_copy(bands_hbm.at[0], bands, arrived.at[1]),
+        pltpu.make_async_copy(bands_hbm.at[0, 0], bands.at[0], arrived.at[0]),
+        pltpu.make_async_copy(bands_hbm.at[0, 1], bands.at[1], arrived.at[1]),
         pltpu.make_async_copy(margins_hbm.at[0], margins, arrived.at[2]),
     ]
+    copies += [pltpu.make_async_copy(right_hbm.at[v], right.at[v], arrived.at[3 + v]) for v in range(VARS)]
     for copy in copies:
         copy.start()
-    copies[1].wait()
-    copies[2].wait()
+    for copy in copies[:3]:
+        copy.wait()
     below, above = bands[0].astype(F32), bands[1].astype(F32)
     middle = jnp.abs(below) + jnp.abs(above) + 0.1 + margins[...].astype(F32)
     for slot, array in enumerate((below, middle, above)):
         put_pitched(lines, slot, array.reshape(128, 128))
-    copies[0].wait()
+    for copy in copies[3:]:
+        copy.wait()
     for v in range(VARS):
         put_pitched(lines, 3 + v, right[v].astype(F32).reshape(128, 128))
     solved = solve_pitched(lines)
@@ -310,7 +312,7 @@
     send_to_all(relation, sent_ref, row, 8)
 
 
-def y_join(got_ref, pair_ref, y_solved_ref, kept_ref, bands_ref, margins_ref, out_ref, lines, row, ordered):
+def y_join(got_ref, pair_ref, y_solved_ref, kept_ref, bands_ref, margins_ref, out_hbm, lines, row, ordered, out, left):
     mine = lax.axis_index("col")
     for position, z in enumerate(DEEP_ORDER):
         ordered[z * 40 : z * 40 + 36, :] = got_ref[position * 36 : position * 36 + 36, :]
@@ -329,8 +331,7 @@
         for v, value in enumerate(with_neighbours(cell, prev, following)):
             lines[v, pl.ds(i, 8, stride=PITCH), :] = value
     below, middle, above = bands_of(bands_ref, margins_ref, 2)
-    ratio_one, ratio_two, reduced = [], [], []
-    fields = [get_pitched(lines, v).T.reshape(8, 16, 128) for v in range(VARS)]
+    lowers, inverses, ratio_one, ratio_two = [], [], [], []
     for i in range(8):
         lower = below[i] + OUTER * ratio_one[i - 2] if i >= 2 else below[i]
         centre = middle[i] + OUTER * ratio_two[i - 2] if i >= 2 else middle[i]
@@ -339,29 +340,31 @@
             centre = centre - lower * ratio_one[i - 1]
             upper = upper - lower * ratio_two[i - 1]
         inverse = 1.0 / centre
-        new = []
-        for v in range(VARS):
-            value = fields[v][i]
-            if i >= 2:
-                value = value + OUTER * reduced[i - 2][v]
-            if i >= 1:
-                value = value - lower * reduced[i - 1][v]
-            new.append(value * inverse)
-        reduced.append(new)
+        lowers.append(lower)
+        inverses.append(inverse)
         ratio_one.append(upper * inverse)
         ratio_two.append(-OUTER * inverse)
-    later = [None, None]
-    for i in range(7, -1, -1):
-        now = []
-        for v in range(VARS):
-            value = reduced[i][v]
-            if later[0] is not None:
-                value = value - ratio_one[i] * later[0][v]
-            if later[1] is not None:
-                value = value - ratio_two[i] * later[1][v]
-            now.append(value)
-            out_ref[v, i] = value
-        later = [now, later[0]]
+    copies = []
+    for v in range(VARS):
+        field = get_pitched(lines, v).T.reshape(8, 16, 128)
+        reduced = []
+        for i in range(8):
+            value = field[i]
+            if i >= 2:
+                value = value + OUTER * reduced[i - 2]
+            if i >= 1:
+                value = value - lowers[i] * reduced[i - 1]
+            reduced.append(value * inverses[i])
+        for i in range(7, -1, -1):
+            if i < 7:
+                reduced[i] = reduced[i] - ratio_one[i] * reduced[i + 1]
+            if i < 6:
+                reduced[i] = reduced[i] - ratio_two[i] * reduced[i + 2]
+            out[v, i] = reduced[i]
+        copies.append(pltpu.make_async_copy(out.at[v], out_hbm.at[v], left.at[v]))
+        copies[v].start()
+    for copy in copies:
+        copy.wait()
 
 
 def call(kernel, outs, scratch):
@@ -388,7 +391,7 @@
             pltpu.VMEM((VARS, 8, 16, 128), jnp.bfloat16),
             pltpu.VMEM((2, 8, 16, 128), jnp.bfloat16),
             pltpu.VMEM((8, 16, 128), jnp.bfloat16),
-            pltpu.SemaphoreType.DMA((3,)),
+            pltpu.SemaphoreType.DMA((3 + VARS,)),
         ],
         compiler_params=PARAMS,
     )(*[pltpu.with_memory_space_constraint(a, pltpu.HBM) for a in (right_side, near_bands, margins)])
@@ -398,10 +401,19 @@
     )(x_solved, exchange(answer, "row", ROWS, 1), near_bands, margins)
     both = lax.all_gather(sent, "col", axis_index_groups=CORES, tiled=True)
     pair, sent = call(y_pair, [(36, 128), (288, 128)], [(36, 128)])(both)
-    (update,) = call(y_join, [(VARS, 8, 16, 128)], [(VARS, 8 * PITCH, 128), (20, 8, 128), (320, 128)])(
-        exchange(sent, "col", DEEP, 4), pair, y_solved, kept, near_bands, margins
-    )
-    return update
+    return pl.pallas_call(
+        y_join,
+        out_specs=pl.BlockSpec(memory_space=pltpu.HBM),
+        out_shape=jax.ShapeDtypeStruct((VARS, 8, 16, 128), F32),
+        scratch_shapes=[
+            pltpu.VMEM((VARS, 8 * PITCH, 128), F32),
+            pltpu.VMEM((20, 8, 128), F32),
+            pltpu.VMEM((320, 128), F32),
+            pltpu.VMEM((VARS, 8, 16, 128), F32),
+            pltpu.SemaphoreType.DMA((VARS,)),
+        ],
+        compiler_params=PARAMS,
+    )(exchange(sent, "col", DEEP, 4), pair, y_solved, kept, near_bands, margins)
 
 
 def solution(mesh):

time: 51.7 us -> 51.8 us (level)
  no operation moved by 1% of the time
where the time goes in v5:
time: 51.8 us; the launch traced here: 51.2 us
  blocking collectives  46.9 us (91%)
  Pallas kernels  4.27 us (8%)
    all_to_all x3, blocking collectives, exchange(): lax.all_to_all(array, axis, 0, 0, tiled=True, axis_index_groups=members)  38.2 us
    all_gather x1, blocking collectives, body(): both = lax.all_gather(sent, 'col', axis_index_groups=CORES, tiled=True)  8.66 us
    pallas_call x1, Pallas kernels, body(): pl.pallas_call(x_local, in_specs=[pl.BlockSpec(memory_space=pltpu.HBM)] *...  1.35 us
    pallas_call x1, Pallas kernels, body(): pl.pallas_call(y_join, out_specs=pl.BlockSpec(memory_space=pltpu.HBM), ou...  1.29 us

profile of v5, /device:TPU:1, one launch (start us, length us, event | category | flops | bytes accessed | tf_op | source)
XLA Modules:
  0.0 51.2 jit_solution(6218641322343766514)
XLA Ops:
  0.0 1.3 %shard_map.37 = (f32[16,9,8,128]{3,2,1,0:T(8,128)S(1)}, f32[288,128]{1,0:T(8,128)S(1)}) custom-call(bf16[5,8,16,128]{3,2,1,0:T(8,128)(2,1)} %right_hbm.1, bf16[3,2,8,16,128]{4,3,2,1,0:T(8,128)(2,1)} %bands_ref.3, bf16[3,8,16,128]{3,2,1,0:T(8,128)(2,1)} %margins_ref.3), custom_call_target="tpu_custom_call" | custom-call | tf_op jit(solution)/shard_map/pallas_call | solution.py:385
  1.4 14.3 %all_to_all.15 = f32[32,9,1,128]{3,2,1,0:T(1,128)S(1)} all-to-all(f32[32,9,1,128]{3,2,1,0:T(1,128)S(1)} %bitcast.12), channel_id=1, replica_groups={{320,336,352,368,256,272,288,304,448,464,480,496,384,400,416,432,64,80,..., dimensions={0} | all-to-all | bytes 294912 | tf_op jit(solution)/shard_map/all_to_all | solution.py:381
  15.7 0.0 copy-start
  15.7 0.9 %shard_map.38 = f32[160,128]{1,0:T(8,128)S(1)} custom-call(f32[288,128]{1,0:T(8,128)S(1)} %bitcast.8), custom_call_target="tpu_custom_call" | custom-call | tf_op jit(solution)/shard_map/pallas_call | solution.py:398
  16.5 0.0 copy-start.1
  16.5 12.1 %all_to_all.16 = f32[32,5,1,128]{3,2,1,0:T(1,128)S(1)} all-to-all(f32[32,5,1,128]{3,2,1,0:T(1,128)S(1)} %bitcast.9), channel_id=1, replica_groups={{320,336,352,368,256,272,288,304,448,464,480,496,384,400,416,432,64,80,..., dimensions={0} | all-to-all | bytes 163840 | tf_op jit(solution)/shard_map/all_to_all | solution.py:381
  28.7 0.0 copy-done
  28.7 0.0 copy-done.1
  28.7 0.7 %shard_map.39 = (f32[16,9,8,128]{3,2,1,0:T(8,128)S(1)}, f32[3,36,8,128]{3,2,1,0:T(8,128)S(1)}, f32[36,128]{1,0:T(8,128)S(1)}) custom-call(f32[16,9,8,128]{3,2,1,0:T(8,128)S(1)} %get-tuple-element.12.x_solved_ref, f32[160,128]{1,0:T(8,128)S(1)} %bitcast.10, bf16[3,2,8,16,128]{4,3,2,1,0:T(8,128)(2,1)S(1)} %copy-done, bf16[3,8,16,128]{3,2,1,0:T(8,128)(2,1)S(1)} %copy-done.1), custom_call_target="tpu_custom_call" | custom-call | tf_op jit(solution)/shard_map/pallas_call | solution.py:399
  29.4 8.7 %all-gather = f32[2,36,128]{2,1,0:T(8,128)S(1)} all-gather(f32[1,36,128]{2,1,0:T(8,128)S(1)} %bitcast.13), channel_id=1, replica_groups={{0,1},{2,3},{4,5},{6,7},{8,9},{10,11},{12,13},{14,15},{16,17},{18,19},{..., dimensions={0}, use_global_device_ids=true | all-gather | bytes 55296 | tf_op jit(solution)/shard_map/all_gather | solution.py:402
  38.0 0.1 shard_map.40
  38.1 11.8 %all_to_all.17 = f32[8,9,4,128]{3,2,1,0:T(4,128)S(1)} all-to-all(f32[8,9,4,128]{3,2,1,0:T(4,128)S(1)} %bitcast.11), channel_id=1, replica_groups={{12,14,10,8,6,4,2,0},{13,15,11,9,7,5,3,1},{28,30,26,24,22,20,18,16},{29..., dimensions={0} | all-to-all | bytes 294912 | tf_op jit(solution)/shard_map/all_to_all | solution.py:381
  49.9 1.3 %shard_map.41 = f32[5,8,16,128]{3,2,1,0:T(8,128)} custom-call(f32[288,128]{1,0:T(8,128)S(1)} %bitcast.7, f32[36,128]{1,0:T(8,128)S(1)} %get-tuple-element.16.pair_ref, f32[16,9,8,128]{3,2,1,0:T(8,128)S(1)} %get-tuple-element.17.y_solved_ref, f32[3,36,8,128]{3,2,1,0:T(8,128)S(1)} %get-tuple-element.18.kept_ref, bf16[3,2,8,16,128]{4,3,2,1,0:T(8,128)(2,1)S(1)} %copy-done, ...), custom_call_target="tpu_custom_call" | custom-call | tf_op jit(solution)/shard_map/pallas_call | solution.py:404
  (1 shorter events, 0.0 us)
Async XLA Ops:
  15.7 13.0 %copy-start = (bf16[3,2,8,16,128]{4,3,2,1,0:T(8,128)(2,1)S(1)}, bf16[3,2,8,16,128]{4,3,2,1,0:T(8,128)(2,1)}, u32[]{:S(2)}) copy-start(bf16[3,2,8,16,128]{4,3,2,1,0:T(8,128)(2,1)} %bands_ref.3) | copy-start | bytes 589828
  16.5 12.1 %copy-start.1 = (bf16[3,8,16,128]{3,2,1,0:T(8,128)(2,1)S(1)}, bf16[3,8,16,128]{3,2,1,0:T(8,128)(2,1)}, u32[]{:S(2)}) copy-start(bf16[3,8,16,128]{3,2,1,0:T(8,128)(2,1)} %margins_ref.3) | copy-start | bytes 294916

commit v6 on v4

--- a/solution.py
+++ b/solution.py
@@ -177,9 +177,9 @@
     return out
 
 
-ROW_MASK, DEEP_ORDER = 20, (6, 7, 5, 4, 3, 2, 1, 0)
+ROW_MASK, DEEP_ORDERS = 20, ((6, 7, 5, 4, 3, 2, 1, 0), (6, 2, 3, 7, 5, 4, 1, 0))
 ROWS = [[k ^ ROW_MASK for k in range(32)]]
-DEEP = [[2 * z + core for z in DEEP_ORDER] for core in range(2)]
+DEEP = [[2 * z + core for z in DEEP_ORDERS[core]] for core in range(2)]
 CORES = [[2 * z, 2 * z + 1] for z in range(8)]
 
 SUB_LEVELS = tuple((0, 1 << bit, 8, False) for bit in range(3))
@@ -312,8 +312,9 @@
 
 def y_join(got_ref, pair_ref, y_solved_ref, kept_ref, bands_ref, margins_ref, out_ref, lines, row, ordered):
     mine = lax.axis_index("col")
-    for position, z in enumerate(DEEP_ORDER):
-        ordered[z * 40 : z * 40 + 36, :] = got_ref[position * 36 : position * 36 + 36, :]
+    for position, (z_zero, z_one) in enumerate(zip(*DEEP_ORDERS)):
+        start = pl.multiple_of((z_zero + (z_one - z_zero) * (mine % 2)) * 40, 8)
+        ordered[pl.ds(start, 36), :] = got_ref[position * 36 : position * 36 + 36, :]
     _, kept = climb([ordered[pl.ds(c, 8, stride=40), :] for c in range(36)], SUB_LEVELS)
     prev, following = descend(kept, SUB_LEVELS, None, None)
     own = own_part(prev + following, mine // 2, row)

time: 51.7 us -> 51.8 us (level)
  no operation moved by 1% of the time
where the time goes in v6:
time: 51.8 us; the launch traced here: 51.3 us
  blocking collectives  46.9 us (91%)
  Pallas kernels  4.32 us (8%)
    all_to_all x3, blocking collectives, exchange(): lax.all_to_all(array, axis, 0, 0, tiled=True, axis_index_groups=members)  38.2 us
    all_gather x1, blocking collectives, body(): both = lax.all_gather(sent, 'col', axis_index_groups=CORES, tiled=True)  8.66 us
    pallas_call x1, Pallas kernels, body(): pl.pallas_call(x_local, in_specs=[pl.BlockSpec(memory_space=pltpu.HBM)] *...  1.38 us
    pallas_call x1, Pallas kernels, body(): call(y_join, [(VARS, 8, 16, 128)], [(VARS, 8 * PITCH, 128), (20, 8, 128),...  1.31 us

profile of v6, /device:TPU:1, one launch (start us, length us, event | category | flops | bytes accessed | tf_op | source)
XLA Modules:
  0.0 51.3 jit_solution(8548130440248750080)
XLA Ops:
  0.0 1.4 %shard_map.37 = (f32[16,9,8,128]{3,2,1,0:T(8,128)S(1)}, f32[288,128]{1,0:T(8,128)S(1)}) custom-call(bf16[5,8,16,128]{3,2,1,0:T(8,128)(2,1)} %right_hbm.1, bf16[3,2,8,16,128]{4,3,2,1,0:T(8,128)(2,1)} %bands_ref.3, bf16[3,8,16,128]{3,2,1,0:T(8,128)(2,1)} %margins_ref.3), custom_call_target="tpu_custom_call" | custom-call | tf_op jit(solution)/shard_map/pallas_call | solution.py:383
  1.4 14.3 %all_to_all.15 = f32[32,9,1,128]{3,2,1,0:T(1,128)S(1)} all-to-all(f32[32,9,1,128]{3,2,1,0:T(1,128)S(1)} %bitcast.12), channel_id=1, replica_groups={{320,336,352,368,256,272,288,304,448,464,480,496,384,400,416,432,64,80,..., dimensions={0} | all-to-all | bytes 294912 | tf_op jit(solution)/shard_map/all_to_all | solution.py:379
  15.7 0.0 copy-start
  15.7 0.9 %shard_map.38 = f32[160,128]{1,0:T(8,128)S(1)} custom-call(f32[288,128]{1,0:T(8,128)S(1)} %bitcast.8), custom_call_target="tpu_custom_call" | custom-call | tf_op jit(solution)/shard_map/pallas_call | solution.py:396
  16.6 0.0 copy-start.1
  16.6 12.1 %all_to_all.16 = f32[32,5,1,128]{3,2,1,0:T(1,128)S(1)} all-to-all(f32[32,5,1,128]{3,2,1,0:T(1,128)S(1)} %bitcast.9), channel_id=1, replica_groups={{320,336,352,368,256,272,288,304,448,464,480,496,384,400,416,432,64,80,..., dimensions={0} | all-to-all | bytes 163840 | tf_op jit(solution)/shard_map/all_to_all | solution.py:379
  28.7 0.0 copy-done
  28.7 0.0 copy-done.1
  28.7 0.7 %shard_map.39 = (f32[16,9,8,128]{3,2,1,0:T(8,128)S(1)}, f32[3,36,8,128]{3,2,1,0:T(8,128)S(1)}, f32[36,128]{1,0:T(8,128)S(1)}) custom-call(f32[16,9,8,128]{3,2,1,0:T(8,128)S(1)} %get-tuple-element.12.x_solved_ref, f32[160,128]{1,0:T(8,128)S(1)} %bitcast.10, bf16[3,2,8,16,128]{4,3,2,1,0:T(8,128)(2,1)S(1)} %copy-done, bf16[3,8,16,128]{3,2,1,0:T(8,128)(2,1)S(1)} %copy-done.1), custom_call_target="tpu_custom_call" | custom-call | tf_op jit(solution)/shard_map/pallas_call | solution.py:397
  29.4 8.7 %all-gather = f32[2,36,128]{2,1,0:T(8,128)S(1)} all-gather(f32[1,36,128]{2,1,0:T(8,128)S(1)} %bitcast.13), channel_id=1, replica_groups={{0,1},{2,3},{4,5},{6,7},{8,9},{10,11},{12,13},{14,15},{16,17},{18,19},{..., dimensions={0}, use_global_device_ids=true | all-gather | bytes 55296 | tf_op jit(solution)/shard_map/all_gather | solution.py:400
  38.1 0.1 shard_map.40
  38.1 11.8 %all_to_all.17 = f32[8,9,4,128]{3,2,1,0:T(4,128)S(1)} all-to-all(f32[8,9,4,128]{3,2,1,0:T(4,128)S(1)} %bitcast.11), channel_id=1, replica_groups={{12,14,10,8,6,4,2,0},{13,5,7,15,11,9,3,1},{28,30,26,24,22,20,18,16},{29..., dimensions={0} | all-to-all | bytes 294912 | tf_op jit(solution)/shard_map/all_to_all | solution.py:379
  49.9 1.3 %shard_map.41 = f32[5,8,16,128]{3,2,1,0:T(8,128)} custom-call(f32[288,128]{1,0:T(8,128)S(1)} %bitcast.7, f32[36,128]{1,0:T(8,128)S(1)} %get-tuple-element.16.pair_ref, f32[16,9,8,128]{3,2,1,0:T(8,128)S(1)} %get-tuple-element.17.y_solved_ref, f32[3,36,8,128]{3,2,1,0:T(8,128)S(1)} %get-tuple-element.18.kept_ref, bf16[3,2,8,16,128]{4,3,2,1,0:T(8,128)(2,1)S(1)} %copy-done, ...), custom_call_target="tpu_custom_call" | custom-call | tf_op jit(solution)/shard_map/pallas_call | solution.py:402
  (1 shorter events, 0.0 us)
Async XLA Ops:
  15.7 13.0 %copy-start = (bf16[3,2,8,16,128]{4,3,2,1,0:T(8,128)(2,1)S(1)}, bf16[3,2,8,16,128]{4,3,2,1,0:T(8,128)(2,1)}, u32[]{:S(2)}) copy-start(bf16[3,2,8,16,128]{4,3,2,1,0:T(8,128)(2,1)} %bands_ref.3) | copy-start | bytes 589828
  16.6 12.1 %copy-start.1 = (bf16[3,8,16,128]{3,2,1,0:T(8,128)(2,1)S(1)}, bf16[3,8,16,128]{3,2,1,0:T(8,128)(2,1)}, u32[]{:S(2)}) copy-start(bf16[3,8,16,128]{3,2,1,0:T(8,128)(2,1)} %margins_ref.3) | copy-start | bytes 294916

commit v7 on v4

--- a/solution.py
+++ b/solution.py
@@ -213,19 +213,21 @@
 
 def x_local(right_hbm, bands_hbm, margins_hbm, solved_ref, sent_ref, lines, right, bands, margins, arrived):
     copies = [
-        pltpu.make_async_copy(right_hbm, right, arrived.at[0]),
-        pltpu.make_async_copy(bands_hbm.at[0], bands, arrived.at[1]),
+        pltpu.make_async_copy(bands_hbm.at[0, 0], bands.at[0], arrived.at[0]),
+        pltpu.make_async_copy(bands_hbm.at[0, 1], bands.at[1], arrived.at[1]),
         pltpu.make_async_copy(margins_hbm.at[0], margins, arrived.at[2]),
     ]
+    copies += [pltpu.make_async_copy(right_hbm.at[v], right.at[v], arrived.at[3 + v]) for v in range(VARS)]
     for copy in copies:
         copy.start()
-    copies[1].wait()
-    copies[2].wait()
+    for copy in copies[:3]:
+        copy.wait()
     below, above = bands[0].astype(F32), bands[1].astype(F32)
     middle = jnp.abs(below) + jnp.abs(above) + 0.1 + margins[...].astype(F32)
     for slot, array in enumerate((below, middle, above)):
         put_pitched(lines, slot, array.reshape(128, 128))
-    copies[0].wait()
+    for copy in copies[3:]:
+        copy.wait()
     for v in range(VARS):
         put_pitched(lines, 3 + v, right[v].astype(F32).reshape(128, 128))
     solved = solve_pitched(lines)
@@ -388,7 +390,7 @@
             pltpu.VMEM((VARS, 8, 16, 128), jnp.bfloat16),
             pltpu.VMEM((2, 8, 16, 128), jnp.bfloat16),
             pltpu.VMEM((8, 16, 128), jnp.bfloat16),
-            pltpu.SemaphoreType.DMA((3,)),
+            pltpu.SemaphoreType.DMA((3 + VARS,)),
         ],
         compiler_params=PARAMS,
     )(*[pltpu.with_memory_space_constraint(a, pltpu.HBM) for a in (right_side, near_bands, margins)])

time: 51.7 us -> 51.8 us (level)
  no operation moved by 1% of the time
where the time goes in v7:
time: 51.8 us; the launch traced here: 51.2 us
  blocking collectives  46.9 us (91%)
  Pallas kernels  4.28 us (8%)
    all_to_all x3, blocking collectives, exchange(): lax.all_to_all(array, axis, 0, 0, tiled=True, axis_index_groups=members)  38.2 us
    all_gather x1, blocking collectives, body(): both = lax.all_gather(sent, 'col', axis_index_groups=CORES, tiled=True)  8.66 us
    pallas_call x1, Pallas kernels, body(): pl.pallas_call(x_local, in_specs=[pl.BlockSpec(memory_space=pltpu.HBM)] *...  1.35 us
    pallas_call x1, Pallas kernels, body(): call(y_join, [(VARS, 8, 16, 128)], [(VARS, 8 * PITCH, 128), (20, 8, 128),...  1.31 us

profile of v7, /device:TPU:1, one launch (start us, length us, event | category | flops | bytes accessed | tf_op | source)
XLA Modules:
  0.0 51.2 jit_solution(12951951788427185514)
XLA Ops:
  0.0 1.3 %shard_map.37 = (f32[16,9,8,128]{3,2,1,0:T(8,128)S(1)}, f32[288,128]{1,0:T(8,128)S(1)}) custom-call(bf16[5,8,16,128]{3,2,1,0:T(8,128)(2,1)} %right_hbm.1, bf16[3,2,8,16,128]{4,3,2,1,0:T(8,128)(2,1)} %bands_ref.3, bf16[3,8,16,128]{3,2,1,0:T(8,128)(2,1)} %margins_ref.3), custom_call_target="tpu_custom_call" | custom-call | tf_op jit(solution)/shard_map/pallas_call | solution.py:384
  1.4 14.3 %all_to_all.15 = f32[32,9,1,128]{3,2,1,0:T(1,128)S(1)} all-to-all(f32[32,9,1,128]{3,2,1,0:T(1,128)S(1)} %bitcast.12), channel_id=1, replica_groups={{320,336,352,368,256,272,288,304,448,464,480,496,384,400,416,432,64,80,..., dimensions={0} | all-to-all | bytes 294912 | tf_op jit(solution)/shard_map/all_to_all | solution.py:380
  15.7 0.0 copy-start
  15.7 0.9 %shard_map.38 = f32[160,128]{1,0:T(8,128)S(1)} custom-call(f32[288,128]{1,0:T(8,128)S(1)} %bitcast.8), custom_call_target="tpu_custom_call" | custom-call | tf_op jit(solution)/shard_map/pallas_call | solution.py:397
  16.5 0.0 copy-start.1
  16.5 12.1 %all_to_all.16 = f32[32,5,1,128]{3,2,1,0:T(1,128)S(1)} all-to-all(f32[32,5,1,128]{3,2,1,0:T(1,128)S(1)} %bitcast.9), channel_id=1, replica_groups={{320,336,352,368,256,272,288,304,448,464,480,496,384,400,416,432,64,80,..., dimensions={0} | all-to-all | bytes 163840 | tf_op jit(solution)/shard_map/all_to_all | solution.py:380
  28.7 0.0 copy-done
  28.7 0.0 copy-done.1
  28.7 0.7 %shard_map.39 = (f32[16,9,8,128]{3,2,1,0:T(8,128)S(1)}, f32[3,36,8,128]{3,2,1,0:T(8,128)S(1)}, f32[36,128]{1,0:T(8,128)S(1)}) custom-call(f32[16,9,8,128]{3,2,1,0:T(8,128)S(1)} %get-tuple-element.12.x_solved_ref, f32[160,128]{1,0:T(8,128)S(1)} %bitcast.10, bf16[3,2,8,16,128]{4,3,2,1,0:T(8,128)(2,1)S(1)} %copy-done, bf16[3,8,16,128]{3,2,1,0:T(8,128)(2,1)S(1)} %copy-done.1), custom_call_target="tpu_custom_call" | custom-call | tf_op jit(solution)/shard_map/pallas_call | solution.py:398
  29.4 8.7 %all-gather = f32[2,36,128]{2,1,0:T(8,128)S(1)} all-gather(f32[1,36,128]{2,1,0:T(8,128)S(1)} %bitcast.13), channel_id=1, replica_groups={{0,1},{2,3},{4,5},{6,7},{8,9},{10,11},{12,13},{14,15},{16,17},{18,19},{..., dimensions={0}, use_global_device_ids=true | all-gather | bytes 55296 | tf_op jit(solution)/shard_map/all_gather | solution.py:401
  38.0 0.1 shard_map.40
  38.1 11.8 %all_to_all.17 = f32[8,9,4,128]{3,2,1,0:T(4,128)S(1)} all-to-all(f32[8,9,4,128]{3,2,1,0:T(4,128)S(1)} %bitcast.11), channel_id=1, replica_groups={{12,14,10,8,6,4,2,0},{13,15,11,9,7,5,3,1},{28,30,26,24,22,20,18,16},{29..., dimensions={0} | all-to-all | bytes 294912 | tf_op jit(solution)/shard_map/all_to_all | solution.py:380
  49.9 1.3 %shard_map.41 = f32[5,8,16,128]{3,2,1,0:T(8,128)} custom-call(f32[288,128]{1,0:T(8,128)S(1)} %bitcast.7, f32[36,128]{1,0:T(8,128)S(1)} %get-tuple-element.16.pair_ref, f32[16,9,8,128]{3,2,1,0:T(8,128)S(1)} %get-tuple-element.17.y_solved_ref, f32[3,36,8,128]{3,2,1,0:T(8,128)S(1)} %get-tuple-element.18.kept_ref, bf16[3,2,8,16,128]{4,3,2,1,0:T(8,128)(2,1)S(1)} %copy-done, ...), custom_call_target="tpu_custom_call" | custom-call | tf_op jit(solution)/shard_map/pallas_call | solution.py:403
  (1 shorter events, 0.0 us)
Async XLA Ops:
  15.7 13.0 %copy-start = (bf16[3,2,8,16,128]{4,3,2,1,0:T(8,128)(2,1)S(1)}, bf16[3,2,8,16,128]{4,3,2,1,0:T(8,128)(2,1)}, u32[]{:S(2)}) copy-start(bf16[3,2,8,16,128]{4,3,2,1,0:T(8,128)(2,1)} %bands_ref.3) | copy-start | bytes 589828
  16.5 12.1 %copy-start.1 = (bf16[3,8,16,128]{3,2,1,0:T(8,128)(2,1)S(1)}, bf16[3,8,16,128]{3,2,1,0:T(8,128)(2,1)}, u32[]{:S(2)}) copy-start(bf16[3,8,16,128]{3,2,1,0:T(8,128)(2,1)} %margins_ref.3) | copy-start | bytes 294916
